TPU v7x, 512 devices: a whole 4x4x16 slice. The times are simulated.
512 devices in a mesh: brick: 128 (over z, y, core), band: 4 (over x).
Axes of the slice: x: 4, y: 4, z: 16, core: 2. Of those that a mesh axis runs over, the one named last changes fastest.
Arguments:
- psi_val: bfloat16 [1024, 256, 2048], P('band', 'brick'), may hold values from -1.1953125 to 1.1953125
- psi_cond: bfloat16 [1024, 256, 2048], P('band', 'brick'), may hold values from -1.1953125 to 1.1953125
- dielectric: float32 [256, 2048], P('brick'), may hold values from 1 to 20
- point_owner: int32 [128], replicated, may hold values from 0 to 127, as said below
- point_cell: int32 [128], replicated, may hold values from 0 to 4095
Outputs:
- pair_field: float32 [128, 256, 2048], P('band', 'brick')
- potential: float32 [128, 256, 2048], P('band', 'brick')
Inputs may be any that keep to these rules, and one draw needn't show every extreme that they name: `point_owner`: no brick owns more than 4 points, and one brick owns exactly 4.
All inputs are finite; a program needn't handle non-finite values.
Results may differ from a plain program's by a relative error of at most 0.0003.
Values may be sent and summed in bfloat16 or wider, within the bound.
A program may use at most 64 MiB of HBM per device.

v0:
```python
import jax
import jax.numpy as jnp
from jax import lax
from jax.sharding import PartitionSpec as P

NZ = 64
SWEEPS = 4


FOURPI = 12.566370614359172
OMEGA = 0.8


def extended(block, sides, width):
    for axis, dim in sides:
        count = lax.axis_size(axis)
        forward = [(i, i + 1) for i in range(count - 1)]
        forward.append((count - 1, 0))
        backward = [(target, source) for source, target in forward]
        low = lax.ppermute(
            lax.slice_in_dim(block, block.shape[dim] - width, None, axis=dim), axis, forward
        )
        high = lax.ppermute(lax.slice_in_dim(block, 0, width, axis=dim), axis, backward)
        block = jnp.concatenate([low, block, high], axis=dim)
    return block


def local(psi_val, psi_cond, dielectric, point_owner, point_cell):
    nbv, cx, plane = psi_val.shape
    nbc = psi_cond.shape[0]
    cells = cx * plane
    npts = point_cell.shape[0]
    nband = lax.axis_size("band")
    fields = npts // nband
    val = psi_val.reshape(nbv, cells)
    cond = psi_cond.reshape(nbc, cells)
    brick_now = lax.axis_index("brick")
    mine = point_owner == brick_now
    picked = lax.broadcasted_iota(jnp.int32, (cells, npts), 0) == point_cell[None, :]
    select = (picked & mine[None, :]).astype(jnp.bfloat16)
    part_v = jnp.dot(val, select, preferred_element_type=jnp.float32)
    part_c = jnp.dot(cond, select, preferred_element_type=jnp.float32)
    part_v, part_c = lax.psum((part_v, part_c), "brick")
    zv = part_v.astype(jnp.bfloat16)
    zc = part_c.astype(jnp.bfloat16)
    contract = (((0,), (0,)), ((), ()))
    term_v = lax.dot_general(zv, val, contract, preferred_element_type=jnp.float32)
    term_c = lax.dot_general(zc, cond, contract, preferred_element_type=jnp.float32)
    summed = lax.psum_scatter(
        jnp.concatenate([term_v, term_c], axis=1), "band", scatter_dimension=0, tiled=True
    )
    pair = summed[:, :cells] * summed[:, cells:]
    pair = pair.reshape(fields, cx, plane)
    depth = lax.broadcasted_iota(jnp.int32, (cx, plane), 1) % NZ
    above = depth < NZ - 1
    below = depth > 0
    eps_wide = extended(dielectric, (("brick", 0),), 1)
    xplus = 0.5 * (dielectric + eps_wide[2:])
    xminus = 0.5 * (dielectric + eps_wide[:-2])
    yplus = 0.5 * (dielectric + jnp.roll(dielectric, -NZ, 1))
    yminus = 0.5 * (dielectric + jnp.roll(dielectric, NZ, 1))
    zplus = 0.5 * (dielectric + jnp.where(above, jnp.roll(dielectric, -1, 1), dielectric))
    zminus = 0.5 * (dielectric + jnp.where(below, jnp.roll(dielectric, 1, 1), dielectric))
    diag = xplus + xminus + yplus + yminus + zplus + zminus
    zplus_cut = jnp.where(above, zplus, 0.0)
    zminus_cut = jnp.where(below, zminus, 0.0)
    rhs = FOURPI * pair
    potential = jnp.zeros_like(pair)
    for sweep in range(SWEEPS):
        widened = extended(potential, (("brick", 1),), 1)
        beside = xplus * widened[:, 2:] + xminus * widened[:, :-2]
        beside = beside + yplus * jnp.roll(potential, -NZ, 2) + yminus * jnp.roll(potential, NZ, 2)
        beside = (
            beside + zplus_cut * jnp.roll(potential, -1, 2) + zminus_cut * jnp.roll(potential, 1, 2)
        )
        applied = diag * potential - beside
        potential = potential + OMEGA * (rhs - applied) / diag
    return (pair, potential)


def solution(mesh):
    return jax.shard_map(
        local,
        mesh=mesh,
        in_specs=(P("band", "brick", None), P("band", "brick", None), P("brick", None), P(), P()),
        out_specs=(P("band", "brick", None), P("band", "brick", None)),
        check_vma=False,
    )
```

profile of v0, /device:TPU:1, one launch (start us, length us, event | category | flops | bytes accessed | tf_op | source)
XLA Modules:
  0.0 628.4 jit_solution(5441378577518195729)
XLA Ops:
  7.2 0.0 reduce-scatter.2.cloned.1.call-start
  7.2 2.5 copy.8
  9.7 0.0 copy-start.3
  9.8 0.8 fusion.9
  10.6 0.8 copy-done.3
  11.3 0.9 copy.7
  12.2 1.4 copy-done.1
  13.6 0.8 fusion.6
  14.4 498.1 %all-reduce.7 = (bf16[256,128]{0,1:T(8,128)(2,1)S(1)}, bf16[256,128]{0,1:T(8,128)(2,1)S(1)}) all-reduce(f32[256,128]{0,1:T(8,128)S(1)} %fusion.9, f32[256,128]{0,1:T(8,128)S(1)} %fusion.6), channel_id=1, replica_groups=mesh['brick'=128,'band'=4] {'brick'}, use_global_device_ids=true, to_apply=%region_1.0 | all-reduce | flops 65536 | bytes 393216 | tf_op jit(solution)/shard_map/psum | solution.py:43
  512.5 0.4 fusion.92
  512.9 1.1 copy-done.2
  514.1 0.4 fusion.93
  514.5 2.3 pad_maximum_fusion
  516.9 0.0 reduce-scatter.2.cloned.1.call-update
  516.9 0.1 broadcast.60
  517.0 3.6 collective-permute-start.3
  520.7 5.9 collective-permute-start.2
  526.6 1.9 collective-permute-start.1
  528.5 7.0 %collective-permute-start = (f32[1,2048]{1,0:T(1,128)S(1)}, f32[1,2048]{1,0:T(1,128)S(1)}, u32[]{:S(2)}, u32[]{:S(2)}) collective-permute-start(f32[1,2048]{1,0:T(1,128)S(1)} %get-tuple-element.47), channel_id=1, source_target_pairs={{4,0},{8,4},{12,8},{16,12},{20,16},{24,20},{28,24},{32,28},{36,32}... | collective-permute-start | bytes 24584 | tf_op jit(solution)/shard_map/ppermute | solution.py:23
  535.5 0.1 fusion.91
  535.6 0.1 fusion.90
  535.6 0.1 fusion.88
  535.7 0.1 broadcast_multiply_fusion.1
  535.8 0.1 fusion.87
  535.9 0.0 collective-permute-done.1
  536.0 0.3 collective-permute-done
  536.3 0.1 broadcast_multiply_fusion.2
  536.4 32.7 %reduce-scatter.2.cloned.1.call-done = f32[32,8192]{1,0:T(8,128)} async-done(((f32[128,8192]{1,0:T(8,128)}), f32[32,8192]{1,0:T(8,128)}) %reduce-scatter.2.cloned.1.call-update) | async-done | bytes 1048592 | tf_op jit(solution)/shard_map/reduce_scatter | solution.py:49
  569.1 1.3 slice_multiply_fusion
  570.3 0.4 reshape.25
  570.8 0.0 copy-start
  570.8 0.0 collective-permute-done.3
  570.8 0.0 collective-permute-done.2
  570.8 1.0 multiply_divide_fusion
  571.8 0.6 fusion.85
  572.5 0.6 fusion.83
  573.1 0.4 fusion.82
  573.5 3.6 collective-permute-start.5
  577.1 2.1 collective-permute-start.4
  579.2 0.1 fusion.86
  579.3 0.1 fusion.84
  579.4 1.0 collective-permute-done.5
  580.4 4.7 collective-permute-done.4
  585.1 4.0 divide_add_fusion.2
  589.2 0.6 fusion.80
  589.8 0.6 fusion.78
  590.4 0.4 fusion.77
  590.8 1.9 collective-permute-start.7
  592.8 4.3 collective-permute-start.6
  597.1 0.1 fusion.81
  597.2 0.1 fusion.79
  597.3 0.0 collective-permute-done.7
  597.3 3.1 collective-permute-done.6
  600.4 4.0 divide_add_fusion.1
  604.5 0.6 fusion.75
  605.1 0.6 fusion.73
  605.7 0.4 fusion.72
  606.2 1.9 collective-permute-start.9
  608.1 7.7 %collective-permute-start.8 = (f32[32,1,2048]{2,1,0:T(1,128)S(1)}, f32[32,1,2048]{2,1,0:T(1,128)S(1)}, u32[]{:S(2)}, u32[]{:S(2)}) collective-permute-start(f32[32,1,2048]{2,1,0:T(1,128)S(1)} %get-tuple-element.12), channel_id=1, source_target_pairs={{4,0},{8,4},{12,8},{16,12},{20,16},{24,20},{28,24},{32,28},{36,32}... | collective-permute-start | bytes 786440 | tf_op jit(solution)/shard_map/ppermute | solution.py:23
  615.7 0.1 fusion.76
  615.8 0.1 fusion.74
  615.9 0.0 collective-permute-done.9
  616.0 0.9 collective-permute-done.8
  616.9 4.7 divide_add_fusion
  (19 shorter events, 0.1 us)
Async XLA Ops:
  7.2 561.9 %reduce-scatter.2.cloned.1.call-start = ((), (), s32[]{:S(2)}) async-start(), calls=%async_computation.1 | async-start | bytes 5242880 | tf_op jit(solution)/shard_map/reduce_scatter | solution.py:49
  7.2 2.5 copy-start.5
  7.2 2.5 copy-start.6
  9.7 1.6 copy-start.3
  12.2 1.4 copy-start.1
  512.5 1.6 copy-start.2
  516.9 9.7 %copy-start.4 = (f32[2,2048]{1,0:T(2,128)S(1)}, f32[2,2048]{1,0:T(2,128)}, u32[]{:S(2)}) copy-start(f32[2,2048]{1,0:T(2,128)} %param.7) | copy-start | bytes 49156
  517.0 53.7 %collective-permute-start.3 = (f32[32,1,2048]{2,1,0:T(1,128)S(1)}, f32[32,1,2048]{2,1,0:T(1,128)S(1)}, u32[]{:S(2)}, u32[]{:S(2)}) collective-permute-start(f32[32,1,2048]{2,1,0:T(1,128)S(1)} %broadcast.60), channel_id=1, source_target_pairs={{0,4},{4,8},{8,12},{12,16},{16,20},{20,24},{24,28},{28,32},{32,36}... | collective-permute-start | bytes 786440 | tf_op jit(solution)/shard_map/ppermute | solution.py:20
  520.7 50.1 %collective-permute-start.2 = (f32[32,1,2048]{2,1,0:T(1,128)S(1)}, f32[32,1,2048]{2,1,0:T(1,128)S(1)}, u32[]{:S(2)}, u32[]{:S(2)}) collective-permute-start(f32[32,1,2048]{2,1,0:T(1,128)S(1)} %broadcast.60), channel_id=1, source_target_pairs={{4,0},{8,4},{12,8},{16,12},{20,16},{24,20},{28,24},{32,28},{36,32}... | collective-permute-start | bytes 786440 | tf_op jit(solution)/shard_map/ppermute | solution.py:23
  526.6 9.4 %collective-permute-start.1 = (f32[1,2048]{1,0:T(1,128)S(1)}, f32[1,2048]{1,0:T(1,128)S(1)}, u32[]{:S(2)}, u32[]{:S(2)}) collective-permute-start(f32[1,2048]{1,0:T(1,128)S(1)} %get-tuple-element.48), channel_id=1, source_target_pairs={{0,4},{4,8},{8,12},{12,16},{16,20},{20,24},{24,28},{28,32},{32,36}... | collective-permute-start | bytes 24584 | tf_op jit(solution)/shard_map/ppermute | solution.py:20
  528.5 7.8 %collective-permute-start = (f32[1,2048]{1,0:T(1,128)S(1)}, f32[1,2048]{1,0:T(1,128)S(1)}, u32[]{:S(2)}, u32[]{:S(2)}) collective-permute-start(f32[1,2048]{1,0:T(1,128)S(1)} %get-tuple-element.47), channel_id=1, source_target_pairs={{4,0},{8,4},{12,8},{16,12},{20,16},{24,20},{28,24},{32,28},{36,32}... | collective-permute-start | bytes 24584 | tf_op jit(solution)/shard_map/ppermute | solution.py:23
  570.8 46.1 %copy-start = (f32[32,2,2048]{2,1,0:T(2,128)}, f32[32,2,2048]{2,1,0:T(2,128)S(1)}, u32[]{:S(2)}) copy-start(f32[32,2,2048]{2,1,0:T(2,128)S(1)} %reshape.25) | copy-start | bytes 1572868
  573.5 6.9 %collective-permute-start.5 = (f32[32,1,2048]{2,1,0:T(1,128)S(1)}, f32[32,1,2048]{2,1,0:T(1,128)S(1)}, u32[]{:S(2)}, u32[]{:S(2)}) collective-permute-start(f32[32,1,2048]{2,1,0:T(1,128)S(1)} %get-tuple-element.33), channel_id=1, source_target_pairs={{0,4},{4,8},{8,12},{12,16},{16,20},{20,24},{24,28},{28,32},{32,36}... | collective-permute-start | bytes 786440 | tf_op jit(solution)/shard_map/ppermute | solution.py:20
  577.1 8.0 %collective-permute-start.4 = (f32[32,1,2048]{2,1,0:T(1,128)S(1)}, f32[32,1,2048]{2,1,0:T(1,128)S(1)}, u32[]{:S(2)}, u32[]{:S(2)}) collective-permute-start(f32[32,1,2048]{2,1,0:T(1,128)S(1)} %get-tuple-element.32), channel_id=1, source_target_pairs={{4,0},{8,4},{12,8},{16,12},{20,16},{24,20},{28,24},{32,28},{36,32}... | collective-permute-start | bytes 786440 | tf_op jit(solution)/shard_map/ppermute | solution.py:23
  590.8 6.5 %collective-permute-start.7 = (f32[32,1,2048]{2,1,0:T(1,128)S(1)}, f32[32,1,2048]{2,1,0:T(1,128)S(1)}, u32[]{:S(2)}, u32[]{:S(2)}) collective-permute-start(f32[32,1,2048]{2,1,0:T(1,128)S(1)} %get-tuple-element.23), channel_id=1, source_target_pairs={{0,4},{4,8},{8,12},{12,16},{16,20},{20,24},{24,28},{28,32},{32,36}... | collective-permute-start | bytes 786440 | tf_op jit(solution)/shard_map/ppermute | solution.py:20
  592.8 7.7 %collective-permute-start.6 = (f32[32,1,2048]{2,1,0:T(1,128)S(1)}, f32[32,1,2048]{2,1,0:T(1,128)S(1)}, u32[]{:S(2)}, u32[]{:S(2)}) collective-permute-start(f32[32,1,2048]{2,1,0:T(1,128)S(1)} %get-tuple-element.22), channel_id=1, source_target_pairs={{4,0},{8,4},{12,8},{16,12},{20,16},{24,20},{28,24},{32,28},{36,32}... | collective-permute-start | bytes 786440 | tf_op jit(solution)/shard_map/ppermute | solution.py:23
  606.2 9.8 %collective-permute-start.9 = (f32[32,1,2048]{2,1,0:T(1,128)S(1)}, f32[32,1,2048]{2,1,0:T(1,128)S(1)}, u32[]{:S(2)}, u32[]{:S(2)}) collective-permute-start(f32[32,1,2048]{2,1,0:T(1,128)S(1)} %get-tuple-element.13), channel_id=1, source_target_pairs={{0,4},{4,8},{8,12},{12,16},{16,20},{20,24},{24,28},{28,32},{32,36}... | collective-permute-start | bytes 786440 | tf_op jit(solution)/shard_map/ppermute | solution.py:20
  608.1 8.8 %collective-permute-start.8 = (f32[32,1,2048]{2,1,0:T(1,128)S(1)}, f32[32,1,2048]{2,1,0:T(1,128)S(1)}, u32[]{:S(2)}, u32[]{:S(2)}) collective-permute-start(f32[32,1,2048]{2,1,0:T(1,128)S(1)} %get-tuple-element.12), channel_id=1, source_target_pairs={{4,0},{8,4},{12,8},{16,12},{20,16},{24,20},{28,24},{32,28},{36,32}... | collective-permute-start | bytes 786440 | tf_op jit(solution)/shard_map/ppermute | solution.py:23
Sparse Core Ops, SparseCore 0:
  517.0 52.0 reduce-scatter.1
where the time goes:
time: 637 us; the launch traced here: 628 us
  blocking collectives  498 us (78%)
  waiting for transfers between devices  42.8 us (7%)
  starting transfers between devices  39.9 us (6%)
  other arithmetic  17.6 us (3%)
  between operations  14.4 us (2%)
  local copies, waits for them, and re-layouts  13.1 us (2%)
    psum x1, blocking collectives, local(): part_v, part_c = lax.psum((part_v, part_c), 'brick')  498 us
    reduce_scatter x1, waiting for transfers between devices, local(): lax.psum_scatter(jnp.concatenate([term_v, term_c], axis=1), 'band', scatt...  32.7 us
    ppermute x5, starting transfers between devices, extended(): lax.ppermute(lax.slice_in_dim(block, 0, width, axis=dim), axis, backward)  26.9 us
    ppermute x5, starting transfers between devices, extended(): lax.ppermute(lax.slice_in_dim(block, block.shape[dim] - width, None, axis...  13 us
    add x3, other arithmetic, local(): potential = potential + OMEGA * (rhs - applied) / diag  12.8 us
  transfers between devices with their start and end apart: 11, of which 6 were waited for; matrix products, arithmetic and copies ran while one was open for 0% of the time, Pallas kernels for 0%

commit v1 on v0

v1 whole, which is shorter than its diff:
```python
import functools

import jax
import jax.numpy as jnp
from jax import lax
from jax.experimental import pallas as pl
from jax.experimental.pallas import tpu as pltpu
from jax.sharding import PartitionSpec as P

NZ = 64
FOURPI = 12.566370614359172
OMEGA = 0.8

CORES = 2
CHIPS_Y = 4
MOST = 4
BLOCK = 4 * MOST
GROUP = 512
LANES = 128
STEP = 32700.0
CODE = 128.0
MESH = pl.DeviceIdType.MESH
F32 = jnp.float32
BF16 = jnp.bfloat16


def iota(shape, dim):
    return lax.broadcasted_iota(jnp.int32, shape, dim)


def to(device):
    return dict(device_id=device, device_id_type=MESH)


def ranks(owner_ref):
    npts = owner_ref.shape[1]
    first_index = iota((npts, npts), 0)
    second_index = iota((npts, npts), 1)
    across = jnp.broadcast_to(owner_ref[...].astype(F32), (npts, npts))
    down = jnp.sum(jnp.where(first_index == second_index, across, 0.0), axis=1, keepdims=True)
    same = across == down
    rank_down = jnp.sum(
        jnp.where(same & (second_index < first_index), 1.0, 0.0), axis=1, keepdims=True
    )
    rank_across = jnp.sum(
        jnp.where(same & (first_index < second_index), 1.0, 0.0), axis=0, keepdims=True
    )
    return down.astype(jnp.int32), rank_down.astype(jnp.int32), rank_across


def points_kernel(owner_ref, cell_ref, val_ref, cond_ref, mine_ref, columns, sem):
    nb, _, plane = val_ref.shape
    brick = lax.axis_index("brick")
    _, _, rank_across = ranks(owner_ref)
    own = owner_ref[...] == brick
    cells = [
        jnp.sum(
            jnp.where(own & (rank_across == j), cell_ref[...].astype(F32), 0.0)
        ).astype(jnp.int32)
        for j in range(MOST)
    ]
    copies = []
    for j in range(MOST):
        slot_plane = jnp.where(cells[j] >= plane, 1, 0)
        column = cells[j] - slot_plane * plane
        start = pl.multiple_of(column // LANES * LANES, LANES)
        for s, psi in enumerate((val_ref, cond_ref)):
            copy = pltpu.make_async_copy(
                psi.at[:, :, pl.ds(start, LANES)], columns.at[2 * j + s], sem.at[j, s]
            )
            copy.start()
            copies.append((copy, j, s, slot_plane, lax.rem(column, LANES)))

    fold = jnp.where(iota((2 * nb, nb), 0) // 2 == iota((2 * nb, nb), 1), 1.0, 0.0).astype(BF16)
    half = nb // 2
    row = iota((BLOCK, LANES), 0)
    lane = iota((BLOCK, LANES), 1)
    wide_row = iota((BLOCK, 2 * nb), 0)
    point_plane = jnp.zeros((BLOCK, 2 * nb), jnp.int32)
    taken = jnp.zeros((BLOCK, 2 * nb), F32)
    for copy, j, s, slot_plane, at in copies:
        copy.wait()
        if s == 0:
            point_plane = jnp.where(lax.rem(wide_row, MOST) == j, slot_plane, point_plane)
        pick = (lax.rem(row, MOST) == j) & (row // (2 * MOST) == s) & (lane == at)
        taken = taken + lax.dot_general(
            jnp.where(pick, 1.0, 0.0).astype(BF16), columns[2 * j + s].reshape(2 * nb, LANES),
            (((1,), (1,)), ((), ())), preferred_element_type=F32,
        )
    keep = lax.rem(iota((BLOCK, 2 * nb), 1), 2) == point_plane
    taken = jnp.dot(jnp.where(keep, taken, 0.0).astype(BF16), fold, preferred_element_type=F32)
    mine = jnp.where(lax.rem(row // MOST, 2) == 0, taken[:, :half], taken[:, half:])
    mine_ref[...] = mine.astype(BF16)


def place_of(brick, nz):
    core = lax.rem(brick, CORES)
    y = lax.rem(brick // CORES, CHIPS_Y)
    z = brick // (CORES * CHIPS_Y)
    return z, y, core


def brick_of(z, y, core):
    return (z * CHIPS_Y + y) * CORES + core


def brick_off(brick, o, bricks):
    return lax.rem(brick + o + bricks, bricks)


def gather_kernel(
    nz, owner_ref, mine_ref, eps_ref, z_ref, coef_ref,
    g_buf, sel, spread, eps_all, eps_rows,
    zs, zr, ys, yr, cs, cr, es, er,
):
    brick = lax.axis_index("brick")
    bricks = nz * CHIPS_Y * CORES
    z, y, core = place_of(brick, nz)
    plane = eps_ref.shape[1]
    npts = owner_ref.shape[1]
    half = LANES
    nb = 2 * half
    groups = min(4, nz)
    per = nz // groups

    barrier = pltpu.get_barrier_semaphore()

    @pl.loop(1, nz)
    def _(dz):
        pl.semaphore_signal(barrier, 1, **to({"brick": brick_of(lax.rem(z + dz, nz), y, core)}))

    for dy in range(1, CHIPS_Y):
        pl.semaphore_signal(
            barrier, 1, **to({"brick": brick_of(z, lax.rem(y + dy, CHIPS_Y), core)})
        )
    pl.semaphore_signal(barrier, 1, **to({"brick": brick_of(z, y, 1 - core)}))
    for o in (-2, -1, 1, 2):
        pl.semaphore_signal(barrier, 1, **to({"brick": brick_off(brick, o, bricks)}))

    g_buf[core, y, z] = mine_ref[...]
    pl.semaphore_wait(barrier, nz - 1 + CHIPS_Y - 1 + 1 + 4)

    def z_copy(dz):
        return pltpu.make_async_remote_copy(
            src_ref=g_buf.at[core, y, z], dst_ref=g_buf.at[core, y, z],
            send_sem=zs.at[dz], recv_sem=zr.at[z],
            **to({"brick": brick_of(lax.rem(z + dz, nz), y, core)})
        )

    @pl.loop(1, nz)
    def _(dz):
        z_copy(dz).start()

    eps_copies = []
    for n, o in enumerate((-2, -1, 1, 2)):
        copy = pltpu.make_async_remote_copy(
            src_ref=eps_ref, dst_ref=eps_all.at[2 - o],
            send_sem=es.at[n], recv_sem=er.at[n], **to({"brick": brick_off(brick, o, bricks)})
        )
        copy.start()
        eps_copies.append(copy)

    owner_down, rank_down, _ = ranks(owner_ref)
    place = ((owner_down & 1) * CHIPS_Y + ((owner_down >> 1) & 3)) * nz + (owner_down >> 3)
    place = place * BLOCK + rank_down

    @pl.loop(0, sel.shape[1] // GROUP)
    def _(n):
        column = iota((npts, GROUP), 1) + n * GROUP
        for q in range(4):
            hit = column == place + q * MOST
            sel[pl.ds(q * npts, npts), pl.ds(pl.multiple_of(n * GROUP, GROUP), GROUP)] = (
                jnp.where(hit, 1.0, 0.0).astype(BF16)
            )

    for p in range(2):
        spread[p] = jnp.where(
            iota((nb, 2 * nb), 1) == 2 * iota((nb, 2 * nb), 0) + p, 1.0, 0.0
        ).astype(BF16)

    def y_copy(g, dy):
        part_of = g_buf.at[core, y, pl.ds(g * per, per)]
        return pltpu.make_async_remote_copy(
            src_ref=part_of, dst_ref=part_of, send_sem=ys.at[dy, g], recv_sem=yr.at[y, g],
            **to({"brick": brick_of(z, lax.rem(y + dy, CHIPS_Y), core)})
        )

    @pl.loop(0, groups)
    def _(g):
        @pl.loop(0, per)
        def _(i):
            source = g * per + i

            @pl.when(source != z)
            def _():
                block = g_buf.at[core, y, source]
                pltpu.make_async_remote_copy(
                    src_ref=block, dst_ref=block, send_sem=zs.at[0], recv_sem=zr.at[source],
                    **to({"brick": brick_of(source, y, core)})
                ).wait_recv()

        for dy in (2, 1, 3):
            y_copy(g, dy).start()

    for copy in eps_copies:
        copy.wait()
    for o in range(5):
        eps_rows[2 * o : 2 * o + 2, :] = eps_ref[...] if o == 2 else eps_all[o]
    here = eps_rows[1:9, :]
    xminus = 0.5 * (here + eps_rows[0:8, :])
    xplus = 0.5 * (here + eps_rows[2:10, :])
    depth = lax.rem(iota((8, plane), 1), NZ)
    above = depth < NZ - 1
    below = depth > 0
    yplus = 0.5 * (here + pltpu.roll(here, plane - NZ, 1))
    yminus = 0.5 * (here + pltpu.roll(here, NZ, 1))
    zplus = 0.5 * (here + jnp.where(above, pltpu.roll(here, plane - 1, 1), here))
    zminus = 0.5 * (here + jnp.where(below, pltpu.roll(here, 1, 1), here))
    scale = OMEGA / (xplus + xminus + yplus + yminus + zplus + zminus)
    faces = (
        xminus, xplus, yminus, yplus,
        jnp.where(below, zminus, 0.0), jnp.where(above, zplus, 0.0), FOURPI,
    )
    for n, face in enumerate(faces):
        coef_ref[n] = scale * face

    def core_copy(g):
        part_of = g_buf.at[core, :, pl.ds(g * per, per)]
        return pltpu.make_async_remote_copy(
            src_ref=part_of, dst_ref=part_of, send_sem=cs.at[g], recv_sem=cr.at[g],
            **to({"brick": brick_of(z, y, 1 - core)})
        )

    @pl.loop(0, groups)
    def _(g):
        @pl.loop(0, CHIPS_Y)
        def _(source):
            @pl.when(source != y)
            def _():
                block = g_buf.at[core, source, pl.ds(g * per, per)]
                pltpu.make_async_remote_copy(
                    src_ref=block, dst_ref=block, send_sem=ys.at[0, g], recv_sem=yr.at[source, g],
                    **to({"brick": brick_of(z, source, core)})
                ).wait_recv()

        core_copy(g).start()

    @pl.loop(0, groups)
    def _(g):
        block = g_buf.at[1 - core, :, pl.ds(g * per, per)]
        pltpu.make_async_remote_copy(
            src_ref=block, dst_ref=block, send_sem=cs.at[g], recv_sem=cr.at[g],
            **to({"brick": brick_of(z, y, 1 - core)})
        ).wait_recv()

    found = jnp.dot(
        sel[...], g_buf[...].reshape(sel.shape[1], LANES), preferred_element_type=F32
    ).astype(BF16)
    for s in range(2):
        for p in range(2):
            low = found[2 * s * npts : (2 * s + 1) * npts, :]
            high = found[(2 * s + 1) * npts : (2 * s + 2) * npts, :]
            z_ref[s, p * npts : (p + 1) * npts, :] = (
                jnp.dot(low, spread[p, :half, :], preferred_element_type=F32)
                + jnp.dot(high, spread[p, half:, :], preferred_element_type=F32)
            ).astype(BF16)

    @pl.loop(1, nz)
    def _(dz):
        z_copy(dz).wait_send()

    @pl.loop(0, groups)
    def _(g):
        for dy in range(1, CHIPS_Y):
            y_copy(g, dy).wait_send()
        core_copy(g).wait_send()


def sums_kernel(
    nz, nx, z_ref, coef_ref, val_ref, cond_ref, pair_ref, pot_ref,
    x_buf, coef, part, out_q, in_q, field, first, second, third, result,
    load_sem, xs, xr, hs, hr, out_sem,
):
    brick = lax.axis_index("brick")
    band = lax.axis_index("band")
    bricks = nz * CHIPS_Y * CORES
    nb8, _, _, plane = val_ref.shape
    nb = nb8 * 8
    npts = z_ref.shape[1] // 2
    fields = npts // nx
    chunks = fields // 8
    tiles = plane // LANES
    parts = plane // GROUP

    def band_off(o):
        return lax.rem(band + o, nx)

    loads = []
    for s, psi in enumerate((val_ref, cond_ref)):
        for i in range(8):
            copy = pltpu.make_async_copy(
                psi.at[:, i], x_buf.at[s, :, 2 * i : 2 * i + 2, :], load_sem.at[s, i]
            )
            copy.start()
            loads.append(copy)

    barrier = pltpu.get_barrier_semaphore()
    for dx in (1, 3):
        pl.semaphore_signal(barrier, 1, **to({"band": band_off(dx)}))
    for o in (-2, -1, 1, 2):
        pl.semaphore_signal(barrier, 1, **to({"brick": brick_off(brick, o, bricks)}))

    @pl.loop(0, 7)
    def _(n):
        rows = coef_ref[n]
        for e in range(8):
            coef[n, e] = jnp.broadcast_to(rows[e : e + 1, :], (8, plane))

    for copy in loads:
        copy.wait()

    @pl.loop(0, parts)
    def _(n):
        at = pl.ds(pl.multiple_of(n * GROUP, GROUP), GROUP)
        for s in range(2):
            got = jnp.dot(
                z_ref[s], x_buf[s, :, :, at].reshape(2 * nb, GROUP), preferred_element_type=F32
            )
            part[s, :, :, at] = got.reshape(2, npts, GROUP)

    pl.semaphore_wait(barrier, 6)

    code_lane = iota((16, LANES), 1)

    def pack(values_at, slot, k):
        codes = jnp.zeros((16, LANES), F32)
        for n in range(parts):
            at = slice(n * GROUP, (n + 1) * GROUP)
            values = values_at(n)
            most = jnp.max(jnp.abs(values), axis=1, keepdims=True)
            code = jnp.ceil(jnp.log2(jnp.maximum(most, 1e-30)) * CODE)
            codes = jnp.where(code_lane == n, code, codes)
            whole = jnp.round(values * (STEP * jnp.exp2(code * (-1.0 / CODE))))
            out_q[slot, k, :, at] = whole.astype(jnp.int32).astype(jnp.int16)
        out_q[slot, k, :, plane:] = codes.astype(jnp.int32).astype(jnp.int16)

    def unpacker(slot, k):
        scales = jnp.exp2(in_q[slot, k, :, plane:].astype(jnp.int32).astype(F32) * (1.0 / CODE))
        scales = scales * (1.0 / STEP)

        def values_at(n):
            got = in_q[slot, k, :, n * GROUP : (n + 1) * GROUP].astype(jnp.int32).astype(F32)
            return got * scales[:, n : n + 1]

        return values_at

    def held(target, p, k):
        start = pl.multiple_of(target * fields + k * 8, 8)

        def values_at(n):
            at = slice(n * GROUP, (n + 1) * GROUP)
            return jnp.concatenate(
                [part[0, p, pl.ds(start, 8), at], part[1, p, pl.ds(start, 8), at]], axis=0
            )

        return values_at

    up, down, across = band_off(1), band_off(3), band_off(2)
    heading = (up, down, up, down, up, down)

    def x_copy(k, slot):
        return pltpu.make_async_remote_copy(
            src_ref=out_q.at[slot, k], dst_ref=in_q.at[slot, k],
            send_sem=xs.at[slot, k], recv_sem=xr.at[slot, k], **to({"band": heading[slot]})
        )

    def join(k):
        for way in range(2):
            x_copy(k, way).wait_recv()
            mine_at, got_at = held(heading[way], way, k), unpacker(way, k)
            pack(lambda n: mine_at(n) + got_at(n), 4 + way, k)
            x_copy(k, 4 + way).start()

    @pl.loop(0, chunks)
    def _(k):
        for way in range(2):
            pack(held(across, way, k), way, k)
            x_copy(k, way).start()
        for way in range(2):
            pack(held(heading[way], 1 - way, k), 2 + way, k)
            x_copy(k, 2 + way).start()

        @pl.when(k > 0)
        def _():
            join(k - 1)

    join(chunks - 1)

    sides = ((-2, 3, 1, 7), (-1, 3, 2, 5), (1, 3, 2, 1), (2, 4, 1, 0))

    def h_copy(k, n):
        o, source, count, target = sides[n]
        return pltpu.make_async_remote_copy(
            src_ref=field.at[k, source : source + count],
            dst_ref=field.at[k, target : target + count],
            send_sem=hs.at[k, n], recv_sem=hr.at[k, n], **to({"brick": brick_off(brick, o, bricks)})
        )

    def out_copy(k, p, which):
        source = field.at[k, 3 + p] if which == 0 else result.at[k, p]
        target = (pair_ref, pot_ref)[which].at[pl.ds(pl.multiple_of(k * 8, 8), 8), p, :]
        return pltpu.make_async_copy(source, target, out_sem.at[k, p, which])

    def product(k):
        for p in range(2):
            x_copy(k, 3 - p).wait_recv()
            x_copy(k, 4 + p).wait_recv()
            parts_at = (held(band, p, k), unpacker(3 - p, k), unpacker(4 + p, k))
            for n in range(parts):
                total = sum(values_at(n) for values_at in parts_at)
                pair = total[:8, :] * total[8:, :]
                field[k, 3 + p, :, n * GROUP : (n + 1) * GROUP] = pair
            out_copy(k, p, 0).start()

    low_half = iota((8, LANES), 1) < NZ

    def sweep(k, source, target, e):
        tile_at = [pl.ds(t * LANES, LANES) for t in range(tiles)]
        swapped = [pltpu.roll(source[e, :, at], NZ, 1) for at in tile_at]
        for t, at in enumerate(tile_at):
            v = source[e, :, at]
            new = (1.0 - OMEGA) * v + first[e, :, at]
            new = new + coef[0, e, :, at] * source[e - 1, :, at]
            new = new + coef[1, e, :, at] * source[e + 1, :, at]
            before = swapped[(t - 1) % tiles]
            after = swapped[(t + 1) % tiles]
            new = new + coef[2, e, :, at] * jnp.where(low_half, before, swapped[t])
            new = new + coef[3, e, :, at] * jnp.where(low_half, swapped[t], after)
            new = new + coef[4, e, :, at] * pltpu.roll(v, 1, 1)
            new = new + coef[5, e, :, at] * pltpu.roll(v, LANES - 1, 1)
            target(e, at, new)

    def sweeps(k):
        for n in range(4):
            h_copy(k, n).wait_recv()

        @pl.loop(0, 8)
        def _(e):
            first[e] = coef[6, e, :, :] * field[k, e]

        def into(ref):
            def store(e, at, new):
                ref[e, :, at] = new
            return store

        def into_result(e, at, new):
            result[k, e - 3, :, at] = new

        pl.loop(1, 7)(lambda e: sweep(k, first, into(second), e))
        pl.loop(2, 6)(lambda e: sweep(k, second, into(third), e))
        pl.loop(3, 5)(lambda e: sweep(k, third, into_result, e))
        for p in range(2):
            out_copy(k, p, 1).start()

    @pl.loop(0, chunks)
    def _(k):
        product(k)
        for n in range(4):
            h_copy(k, n).start()

        @pl.when(k > 0)
        def _():
            sweeps(k - 1)

    sweeps(chunks - 1)

    @pl.loop(0, chunks)
    def _(k):
        for slot in range(6):
            x_copy(k, slot).wait_send()
        for n in range(4):
            h_copy(k, n).wait_send()
        for p in range(2):
            for which in range(2):
                out_copy(k, p, which).wait()


def local(bricks, nx, psi_val, psi_cond, dielectric, point_owner, point_cell):
    nb, _, plane = psi_val.shape
    npts = point_owner.shape[0]
    nz = bricks // (CHIPS_Y * CORES)
    groups = min(4, nz)
    fields = npts // nx
    chunks = fields // 8
    rows = bricks * BLOCK
    owner = point_owner.reshape(1, npts)

    vmem = pl.BlockSpec(memory_space=pltpu.VMEM)
    hbm = pl.BlockSpec(memory_space=pl.ANY)
    dma = pltpu.SemaphoreType.DMA
    mine = pl.pallas_call(
        points_kernel,
        out_shape=jax.ShapeDtypeStruct((BLOCK, LANES), BF16),
        in_specs=[vmem, vmem, hbm, hbm],
        out_specs=vmem,
        scratch_shapes=[pltpu.VMEM((2 * MOST + 1, nb, 2, LANES), BF16), dma((MOST, 2))],
        compiler_params=pltpu.CompilerParams(vmem_limit_bytes=58 << 20),
        name="points",
    )(owner, point_cell.reshape(1, npts), psi_val, psi_cond)
    weights, coef = pl.pallas_call(
        functools.partial(gather_kernel, nz),
        out_shape=[
            jax.ShapeDtypeStruct((2, 2 * npts, 2 * nb), BF16),
            jax.ShapeDtypeStruct((7, 8, plane), F32),
        ],
        in_specs=[vmem, vmem, vmem],
        out_specs=[vmem, vmem],
        scratch_shapes=[
            pltpu.VMEM((CORES, CHIPS_Y, nz, BLOCK, LANES), BF16),
            pltpu.VMEM((4 * npts, rows), BF16),
            pltpu.VMEM((2, nb, 2 * nb), BF16),
            pltpu.VMEM((5, 2, plane), F32),
            pltpu.VMEM((16, plane), F32),
            dma((nz,)), dma((nz,)),
            dma((CHIPS_Y, groups)), dma((CHIPS_Y, groups)),
            dma((groups,)), dma((groups,)),
            dma((4,)), dma((4,)),
        ],
        compiler_params=pltpu.CompilerParams(
            collective_id=0, has_side_effects=True, vmem_limit_bytes=24 << 20
        ),
        name="gather",
    )(owner, mine, dielectric)
    return pl.pallas_call(
        functools.partial(sums_kernel, nz, nx),
        out_shape=[jax.ShapeDtypeStruct((fields, 2, plane), F32)] * 2,
        in_specs=[vmem, vmem, hbm, hbm],
        out_specs=[hbm, hbm],
        scratch_shapes=[
            pltpu.VMEM((2, nb // 8, 16, plane), BF16),
            pltpu.VMEM((7, 8, 8, plane), F32),
            pltpu.VMEM((2, 2, npts, plane), F32),
            pltpu.VMEM((6, chunks, 16, plane + LANES), jnp.int16),
            pltpu.VMEM((6, chunks, 16, plane + LANES), jnp.int16),
            pltpu.VMEM((chunks, 8, 8, plane), F32),
            pltpu.VMEM((8, 8, plane), F32),
            pltpu.VMEM((8, 8, plane), F32),
            pltpu.VMEM((8, 8, plane), F32),
            pltpu.VMEM((chunks, 2, 8, plane), F32),
            dma((2, 8)),
            dma((6, chunks)), dma((6, chunks)),
            dma((chunks, 4)), dma((chunks, 4)),
            dma((chunks, 2, 2)),
        ],
        compiler_params=pltpu.CompilerParams(
            collective_id=1, has_side_effects=True, vmem_limit_bytes=40 << 20
        ),
        name="sums",
    )(
        weights, coef, psi_val.reshape(nb // 8, 8, 2, plane),
        psi_cond.reshape(nb // 8, 8, 2, plane),
    )


def solution(mesh):
    return jax.shard_map(
        functools.partial(local, mesh.shape["brick"], mesh.shape["band"]),
        mesh=mesh,
        in_specs=(P("band", "brick", None), P("band", "brick", None), P("brick", None), P(), P()),
        out_specs=(P("band", "brick", None), P("band", "brick", None)),
        check_vma=False,
    )
```

time: 637 us -> 82.6 us (0.13); the launches traced: 628 us -> 82.4 us
  blocking collectives: 498 us -> 0 us
  Pallas kernels: 0 us -> 78.7 us
  waiting for transfers between devices: 42.8 us -> 0 us
  starting transfers between devices: 39.9 us -> 0 us
  other arithmetic: 17.6 us -> 0 us
  between operations: 14.4 us -> 0.71 us
  local copies, waits for them, and re-layouts: 13.1 us -> 3 us
    psum x1 -> x0, blocking collectives: 498 us -> none  [local(): part_v, part_c = lax.psum((part_v, part_c), 'brick')]
    pallas_call x0 -> x3, Pallas kernels: none -> 78.7 us  [the longest x1 43.7 us: local(): pl.pallas_call(functools.partial(sums_kernel, nz, nx), out_shape=[jax.Sha...]
    ppermute x10 -> x0, starting transfers between devices: 39.9 us -> none  [the longest x5 26.9 us: extended(): lax.ppermute(lax.slice_in_dim(block, 0, width, axis=dim), axis, backward)]
    reduce_scatter x1 -> x0, waiting for transfers between devices: 32.7 us -> none  [local(): lax.psum_scatter(jnp.concatenate([term_v, term_c], axis=1), 'band', scatt...]
    add x3 -> x0, other arithmetic: 12.8 us -> none  [local(): potential = potential + OMEGA * (rhs - applied) / diag]
    ppermute x10 -> x0, waiting for transfers between devices: 10.1 us -> none  [the longest x5 9.08 us: extended(): lax.ppermute(lax.slice_in_dim(block, 0, width, axis=dim), axis, backward)]
  transfers between devices with their start and end apart: 11 -> 0, of which waited for: 6 -> 0; matrix products, arithmetic and copies ran while one was open for 0% -> 0% of each run, Pallas kernels for 0% -> 0%
where the time goes in v1:
time: 82.6 us; the launch traced here: 82.4 us
  Pallas kernels  78.7 us (95%)
  local copies, waits for them, and re-layouts  3 us (4%)
    pallas_call x1, Pallas kernels, local(): pl.pallas_call(functools.partial(sums_kernel, nz, nx), out_shape=[jax.Sha...  43.7 us
    pallas_call x1, Pallas kernels, local(): pl.pallas_call(functools.partial(gather_kernel, nz), out_shape=[jax.Shape...  31.2 us
    pallas_call x1, Pallas kernels, local(): pl.pallas_call(points_kernel, out_shape=jax.ShapeDtypeStruct((BLOCK, LANE...  3.72 us
    unnamed x12, local copies, waits for them, and re-layouts  3 us

profile of v1, /device:TPU:1, one launch (start us, length us, event | category | flops | bytes accessed | tf_op | source)
XLA Modules:
  0.0 82.4 jit_solution(16846860329443375601)
XLA Ops:
  0.6 0.0 copy-start.4
  0.6 0.0 copy-start
  0.7 0.0 copy-start.1
  0.7 3.7 %points.1.mine_ref = bf16[16,128]{1,0:T(8,128)(2,1)} custom-call(s32[1,128]{1,0:T(1,128)} %bitcast.6, s32[1,128]{1,0:T(1,128)} %bitcast.8, bf16[256,2,2048]{2,1,0:T(2,128)(2,1)} %val_ref.1, bf16[256,2,2048]{2,1,0:T(2,128)(2,1)} %cond_ref.1), custom_call_target="tpu_custom_call" | custom-call | tf_op jit(solution)/shard_map/points/pallas_call | solution.py:501
  4.4 0.0 copy-done.4
  4.4 0.0 copy-start.2
  4.4 0.7 copy-done.2
  5.1 0.0 copy-start.3
  5.1 0.7 copy-done.3
  5.8 31.2 %gather.1 = (bf16[2,256,512]{2,1,0:T(8,128)(2,1)S(1)}, f32[7,8,2048]{2,1,0:T(8,128)S(1)}) custom-call(s32[1,128]{1,0:T(1,128)S(1)} %bitcast.7, bf16[16,128]{1,0:T(8,128)(2,1)S(1)} %copy-done.3, f32[2,2048]{1,0:T(2,128)S(1)} %copy-done.2), custom_call_target="tpu_custom_call" | custom-call | tf_op jit(solution)/shard_map/gather/pallas_call | solution.py:510
  37.0 0.0 copy-done
  37.0 0.0 copy-done.1
  37.0 43.7 %sums.1 = (f32[32,2,2048]{2,1,0:T(2,128)S(1)}, f32[32,2,2048]{2,1,0:T(2,128)S(1)}) custom-call(bf16[2,256,512]{2,1,0:T(8,128)(2,1)S(1)} %get-tuple-element.4.z_ref, f32[7,8,2048]{2,1,0:T(8,128)S(1)} %get-tuple-element.5.coef_ref, bf16[32,8,2,2048]{3,2,1,0:T(2,128)(2,1)S(1)} %bitcast.4, bf16[32,8,2,2048]{3,2,1,0:T(2,128)(2,1)S(1)} %bitcast.5), custom_call_target="tpu_custom_call" | custom-call | tf_op jit(solution)/shard_map/sums/pallas_call | solution.py:534
  80.8 0.8 copy.9
  81.6 0.8 copy.10
Async XLA Ops:
  0.6 3.8 %copy-start.4 = (s32[128]{0:T(128)S(1)}, s32[128]{0:T(128)}, u32[]{:S(2)}) copy-start(s32[128]{0:T(128)} %param.8) | copy-start | bytes 1540
  0.6 36.4 %copy-start = (bf16[256,2,2048]{2,1,0:T(2,128)(2,1)S(1)}, bf16[256,2,2048]{2,1,0:T(2,128)(2,1)}, u32[]{:S(2)}) copy-start(bf16[256,2,2048]{2,1,0:T(2,128)(2,1)} %val_ref.1) | copy-start | bytes 6291460
  0.7 36.4 %copy-start.1 = (bf16[256,2,2048]{2,1,0:T(2,128)(2,1)S(1)}, bf16[256,2,2048]{2,1,0:T(2,128)(2,1)}, u32[]{:S(2)}) copy-start(bf16[256,2,2048]{2,1,0:T(2,128)(2,1)} %cond_ref.1) | copy-start | bytes 6291460
  4.4 0.7 copy-start.2
  5.1 0.7 copy-start.3

commit v2 on v1

v2 whole, which is shorter than its diff:
```python
import functools

import jax
import jax.numpy as jnp
from jax import lax
from jax.experimental import pallas as pl
from jax.experimental.pallas import tpu as pltpu
from jax.sharding import PartitionSpec as P

NZ = 64
FOURPI = 12.566370614359172
OMEGA = 0.8

CORES = 2
CHIPS_Y = 4
MOST = 4
BLOCK = 4 * MOST
GROUP = 512
LANES = 128
STEP = 32700.0
CODE = 128.0
MESH = pl.DeviceIdType.MESH
F32 = jnp.float32
BF16 = jnp.bfloat16


def iota(shape, dim):
    return lax.broadcasted_iota(jnp.int32, shape, dim)


def to(device):
    return dict(device_id=device, device_id_type=MESH)


def ranks(owners):
    npts = owners.shape[1]
    first_index = iota((npts, npts), 0)
    second_index = iota((npts, npts), 1)
    across = jnp.broadcast_to(owners.astype(F32), (npts, npts))
    down = jnp.sum(jnp.where(first_index == second_index, across, 0.0), axis=1, keepdims=True)
    same = across == down
    rank_down = jnp.sum(
        jnp.where(same & (second_index < first_index), 1.0, 0.0), axis=1, keepdims=True
    )
    rank_across = jnp.sum(
        jnp.where(same & (first_index < second_index), 1.0, 0.0), axis=0, keepdims=True
    )
    return down.astype(jnp.int32), rank_down.astype(jnp.int32), rank_across


def points_kernel(
    owner_ref, cell_ref, eps_ref, val_ref, cond_ref, table_ref, columns, sem
):
    nb, _, plane = val_ref.shape
    brick = lax.axis_index("brick")
    _, _, rank_across = ranks(owner_ref[...])
    own = owner_ref[...] == brick
    cells = [
        jnp.sum(
            jnp.where(own & (rank_across == j), cell_ref[...].astype(F32), 0.0)
        ).astype(jnp.int32)
        for j in range(MOST)
    ]
    copies = []
    for j in range(MOST):
        slot_plane = jnp.where(cells[j] >= plane, 1, 0)
        column = cells[j] - slot_plane * plane
        start = pl.multiple_of(column // LANES * LANES, LANES)
        for s, psi in enumerate((val_ref, cond_ref)):
            copy = pltpu.make_async_copy(
                psi.at[:, :, pl.ds(start, LANES)], columns.at[2 * j + s], sem.at[j, s]
            )
            copy.start()
            copies.append((copy, j, s, slot_plane, lax.rem(column, LANES)))

    table_ref[...] = jnp.zeros_like(table_ref)
    table_ref[0:2, :plane] = eps_ref[...]
    table_ref[2:3, : owner_ref.shape[1]] = owner_ref[...].astype(F32)

    fold = jnp.where(iota((2 * nb, nb), 0) // 2 == iota((2 * nb, nb), 1), 1.0, 0.0).astype(BF16)
    half = nb // 2
    row = iota((BLOCK, LANES), 0)
    lane = iota((BLOCK, LANES), 1)
    wide_row = iota((BLOCK, 2 * nb), 0)
    point_plane = jnp.zeros((BLOCK, 2 * nb), jnp.int32)
    taken = jnp.zeros((BLOCK, 2 * nb), F32)
    for copy, j, s, slot_plane, at in copies:
        copy.wait()
        if s == 0:
            point_plane = jnp.where(lax.rem(wide_row, MOST) == j, slot_plane, point_plane)
        pick = (lax.rem(row, MOST) == j) & (row // (2 * MOST) == s) & (lane == at)
        taken = taken + lax.dot_general(
            jnp.where(pick, 1.0, 0.0).astype(BF16), columns[2 * j + s].reshape(2 * nb, LANES),
            (((1,), (1,)), ((), ())), preferred_element_type=F32,
        )
    keep = lax.rem(iota((BLOCK, 2 * nb), 1), 2) == point_plane
    taken = jnp.dot(jnp.where(keep, taken, 0.0).astype(BF16), fold, preferred_element_type=F32)
    mine = jnp.where(lax.rem(row // MOST, 2) == 0, taken[:, :half], taken[:, half:])
    table_ref[:, plane : plane + LANES] = mine[:8, :]
    table_ref[:, plane + LANES :] = mine[8:, :]


def kernel(
    nz, nx,
    table_ref, val_ref, cond_ref,
    pair_ref, pot_ref,
    x_buf, g_buf, sel, found, spread, z_buf, part, out_q, in_q, eps_all, eps_rows, coef,
    field, first, second, third, result,
    load_sem, zs, zr, ys, yr, cs, cr, xs, xr, hs, hr, es, er, out_sem,
):
    brick = lax.axis_index("brick")
    band = lax.axis_index("band")
    bricks = nz * CHIPS_Y * CORES
    core = lax.rem(brick, CORES)
    y = lax.rem(brick // CORES, CHIPS_Y)
    z = brick // (CORES * CHIPS_Y)
    nb8, _, _, plane = val_ref.shape
    nb = nb8 * 8
    npts = part.shape[2]
    owners = table_ref[2:3, :npts]
    fields = npts // nx
    chunks = fields // 8
    groups = min(4, nz)
    per = nz // groups
    tiles = plane // LANES
    parts = plane // GROUP

    def brick_at(zz, yy, cc):
        return (zz * CHIPS_Y + yy) * CORES + cc

    def brick_off(o):
        return lax.rem(brick + o + bricks, bricks)

    def band_off(o):
        return lax.rem(band + o, nx)

    loads = []
    for s, psi in enumerate((val_ref, cond_ref)):
        for i in range(8):
            copy = pltpu.make_async_copy(
                psi.at[:, i], x_buf.at[s, :, 2 * i : 2 * i + 2, :], load_sem.at[s, i]
            )
            copy.start()
            loads.append(copy)

    barrier = pltpu.get_barrier_semaphore()

    @pl.loop(1, nz)
    def _(dz):
        pl.semaphore_signal(barrier, 1, **to({"brick": brick_at(lax.rem(z + dz, nz), y, core)}))

    for dy in (1, 3):
        pl.semaphore_signal(
            barrier, 1, **to({"brick": brick_at(z, lax.rem(y + dy, CHIPS_Y), core)})
        )
    pl.semaphore_signal(barrier, 1, **to({"brick": brick_at(z, y, 1 - core)}))
    for dx in (1, 3):
        pl.semaphore_signal(barrier, 1, **to({"band": band_off(dx)}))
    for o in (-2, -1, 1, 2):
        pl.semaphore_signal(barrier, 1, **to({"brick": brick_off(o)}))

    g_buf[core, y, z] = jnp.concatenate(
        [table_ref[:, plane : plane + LANES], table_ref[:, plane + LANES :]], axis=0
    ).astype(BF16)
    eps_all[2] = table_ref[0:2, :plane]
    pl.semaphore_wait(barrier, nz - 1 + 2 + 1 + 2 + 4)

    def z_copy(dz):
        return pltpu.make_async_remote_copy(
            src_ref=g_buf.at[core, y, z], dst_ref=g_buf.at[core, y, z],
            send_sem=zs.at[dz], recv_sem=zr.at[z],
            **to({"brick": brick_at(lax.rem(z + dz, nz), y, core)})
        )

    for dz in sorted(range(1, nz), key=lambda d: -min(d, nz - d)):
        z_copy(dz).start()

    eps_copies = []
    for n, o in enumerate((-2, -1, 1, 2)):
        copy = pltpu.make_async_remote_copy(
            src_ref=eps_all.at[2], dst_ref=eps_all.at[2 - o],
            send_sem=es.at[n], recv_sem=er.at[n], **to({"brick": brick_off(o)})
        )
        copy.start()
        eps_copies.append(copy)

    owner_down, rank_down, _ = ranks(owners)
    owner_z = owner_down >> 3
    group_down = jnp.zeros_like(owner_z)
    for g in range(1, groups):
        group_down = group_down + jnp.where(owner_z >= g * per, 1, 0)
    place = ((owner_down & 1) * groups + group_down) * CHIPS_Y + ((owner_down >> 1) & 3)
    place = (place * per + owner_z - group_down * per) * BLOCK + rank_down

    @pl.loop(0, sel.shape[1] // GROUP)
    def _(n):
        column = iota((npts, GROUP), 1) + n * GROUP
        for q in range(4):
            hit = column == place + q * MOST
            sel[pl.ds(q * npts, npts), pl.ds(pl.multiple_of(n * GROUP, GROUP), GROUP)] = (
                jnp.where(hit, 1.0, 0.0).astype(BF16)
            )

    for p in range(2):
        spread[:, 2 * nb * p : 2 * nb * (p + 1)] = jnp.where(
            iota((nb, 2 * nb), 1) == 2 * iota((nb, 2 * nb), 0) + p, 1.0, 0.0
        ).astype(BF16)

    y_up, y_down = lax.rem(y + 1, CHIPS_Y), lax.rem(y + 3, CHIPS_Y)

    def y_copy(g, way):
        odd = lax.rem(g, 2)
        source = y if way < 2 else jnp.where(odd == 1, y_up, y_down)
        target = (y_up, y_down, jnp.where(odd == 1, y_down, y_up))[way]
        part_of = g_buf.at[core, source, pl.ds(g * per, per)]
        return pltpu.make_async_remote_copy(
            src_ref=part_of, dst_ref=part_of, send_sem=ys.at[way, g], recv_sem=yr.at[source, g],
            **to({"brick": brick_at(z, target, core)})
        )

    def y_arrived(source, g):
        block = g_buf.at[core, source, pl.ds(g * per, per)]
        pltpu.make_async_remote_copy(
            src_ref=block, dst_ref=block, send_sem=ys.at[0, g], recv_sem=yr.at[source, g],
            **to({"brick": brick_at(z, source, core)})
        ).wait_recv()

    @pl.loop(0, groups)
    def _(g):
        @pl.loop(0, per)
        def _(i):
            source = g * per + i

            @pl.when(source != z)
            def _():
                block = g_buf.at[core, y, source]
                pltpu.make_async_remote_copy(
                    src_ref=block, dst_ref=block, send_sem=zs.at[0], recv_sem=zr.at[source],
                    **to({"brick": brick_at(source, y, core)})
                ).wait_recv()

        y_copy(g, 0).start()
        y_copy(g, 1).start()

    @pl.loop(0, groups)
    def _(g):
        y_arrived(jnp.where(lax.rem(g, 2) == 1, y_up, y_down), g)
        y_copy(g, 2).start()

    for copy in eps_copies:
        copy.wait()
    for o in range(5):
        eps_rows[2 * o : 2 * o + 2, :] = eps_all[o]
    here = eps_rows[1:9, :]
    xminus = 0.5 * (here + eps_rows[0:8, :])
    xplus = 0.5 * (here + eps_rows[2:10, :])
    depth = lax.rem(iota((8, plane), 1), NZ)
    above = depth < NZ - 1
    below = depth > 0
    yplus = 0.5 * (here + pltpu.roll(here, plane - NZ, 1))
    yminus = 0.5 * (here + pltpu.roll(here, NZ, 1))
    zplus = 0.5 * (here + jnp.where(above, pltpu.roll(here, plane - 1, 1), here))
    zminus = 0.5 * (here + jnp.where(below, pltpu.roll(here, 1, 1), here))
    scale = OMEGA / (xplus + xminus + yplus + yminus + zplus + zminus)
    faces = (
        xminus, xplus, yminus, yplus,
        jnp.where(below, zminus, 0.0), jnp.where(above, zplus, 0.0), FOURPI,
    )
    for n, face in enumerate(faces):
        scaled = scale * face
        for e in range(8):
            coef[n, e] = jnp.broadcast_to(scaled[e : e + 1, :], (8, plane))

    def core_copy(g):
        part_of = g_buf.at[core, :, pl.ds(g * per, per)]
        return pltpu.make_async_remote_copy(
            src_ref=part_of, dst_ref=part_of, send_sem=cs.at[g], recv_sem=cr.at[g],
            **to({"brick": brick_at(z, y, 1 - core)})
        )

    columns_of = CHIPS_Y * per * BLOCK

    def find(c, g):
        rows = g_buf[c, :, pl.ds(g * per, per)].reshape(columns_of, LANES)
        start = pl.multiple_of((c * groups + g) * columns_of, columns_of)
        return jnp.dot(sel[:, pl.ds(start, columns_of)], rows, preferred_element_type=F32)

    found[...] = jnp.zeros_like(found)

    @pl.loop(0, groups)
    def _(g):
        y_arrived(jnp.where(lax.rem(g, 2) == 1, y_down, y_up), g)
        y_arrived(lax.rem(y + 2, CHIPS_Y), g)
        core_copy(g).start()

    @pl.loop(0, groups)
    def _(g):
        found[...] += find(core, g)

    @pl.loop(0, groups)
    def _(g):
        block = g_buf.at[1 - core, :, pl.ds(g * per, per)]
        pltpu.make_async_remote_copy(
            src_ref=block, dst_ref=block, send_sem=cs.at[g], recv_sem=cr.at[g],
            **to({"brick": brick_at(z, y, 1 - core)})
        ).wait_recv()
        found[...] += find(1 - core, g)

    for copy in loads:
        copy.wait()

    for s in range(2):
        at_points = jnp.concatenate(
            [found[(2 * s + i) * npts : (2 * s + i + 1) * npts, :] for i in range(2)], axis=1
        ).astype(BF16)
        wide = jnp.dot(at_points, spread[...], preferred_element_type=F32).astype(BF16)
        for p in range(2):
            z_buf[s, p * npts : (p + 1) * npts, :] = wide[:, 2 * nb * p : 2 * nb * (p + 1)]

    @pl.loop(0, parts)
    def _(n):
        at = pl.ds(pl.multiple_of(n * GROUP, GROUP), GROUP)
        for s in range(2):
            got = jnp.dot(
                z_buf[s], x_buf[s, :, :, at].reshape(2 * nb, GROUP), preferred_element_type=F32
            )
            part[s, :, :, at] = got.reshape(2, npts, GROUP)

    code_lane = iota((16, LANES), 1)

    def pack(values_at, slot, k):
        codes = jnp.zeros((16, LANES), F32)
        for n in range(parts):
            at = slice(n * GROUP, (n + 1) * GROUP)
            values = values_at(n)
            most = jnp.max(jnp.abs(values), axis=1, keepdims=True)
            code = jnp.ceil(jnp.log2(jnp.maximum(most, 1e-30)) * CODE)
            codes = jnp.where(code_lane == n, code, codes)
            whole = jnp.round(values * (STEP * jnp.exp2(code * (-1.0 / CODE))))
            out_q[slot, k, :, at] = whole.astype(jnp.int32).astype(jnp.int16)
        out_q[slot, k, :, plane:] = codes.astype(jnp.int32).astype(jnp.int16)

    def unpacker(slot, k):
        scales = jnp.exp2(in_q[slot, k, :, plane:].astype(jnp.int32).astype(F32) * (1.0 / CODE))
        scales = scales * (1.0 / STEP)

        def values_at(n):
            got = in_q[slot, k, :, n * GROUP : (n + 1) * GROUP].astype(jnp.int32).astype(F32)
            return got * scales[:, n : n + 1]

        return values_at

    def held(target, p, k):
        start = pl.multiple_of(target * fields + k * 8, 8)

        def values_at(n):
            at = slice(n * GROUP, (n + 1) * GROUP)
            return jnp.concatenate(
                [part[0, p, pl.ds(start, 8), at], part[1, p, pl.ds(start, 8), at]], axis=0
            )

        return values_at

    up, down, across = band_off(1), band_off(3), band_off(2)
    heading = (up, down, up, down, up, down)

    def x_copy(k, slot):
        return pltpu.make_async_remote_copy(
            src_ref=out_q.at[slot, k], dst_ref=in_q.at[slot, k],
            send_sem=xs.at[slot, k], recv_sem=xr.at[slot, k], **to({"band": heading[slot]})
        )

    def join(k):
        for way in range(2):
            x_copy(k, way).wait_recv()
            mine_at, got_at = held(heading[way], way, k), unpacker(way, k)
            pack(lambda n: mine_at(n) + got_at(n), 4 + way, k)
            x_copy(k, 4 + way).start()

    def send(k):
        for way in range(2):
            pack(held(across, way, k), way, k)
            x_copy(k, way).start()
        for way in range(2):
            pack(held(heading[way], 1 - way, k), 2 + way, k)
            x_copy(k, 2 + way).start()

    sides = ((-2, 3, 1, 7), (-1, 3, 2, 5), (1, 3, 2, 1), (2, 4, 1, 0))

    def h_copy(k, n):
        o, source, count, target = sides[n]
        return pltpu.make_async_remote_copy(
            src_ref=field.at[k, source : source + count],
            dst_ref=field.at[k, target : target + count],
            send_sem=hs.at[k, n], recv_sem=hr.at[k, n], **to({"brick": brick_off(o)})
        )

    def out_copy(k, p, which):
        source = field.at[k, 3 + p] if which == 0 else result.at[k, p]
        target = (pair_ref, pot_ref)[which].at[pl.ds(pl.multiple_of(k * 8, 8), 8), p, :]
        return pltpu.make_async_copy(source, target, out_sem.at[k, p, which])

    def product(k):
        for p in range(2):
            x_copy(k, 3 - p).wait_recv()
            x_copy(k, 4 + p).wait_recv()
            parts_at = (held(band, p, k), unpacker(3 - p, k), unpacker(4 + p, k))
            for n in range(parts):
                total = sum(values_at(n) for values_at in parts_at)
                pair = total[:8, :] * total[8:, :]
                field[k, 3 + p, :, n * GROUP : (n + 1) * GROUP] = pair
            out_copy(k, p, 0).start()

    low_half = iota((8, LANES), 1) < NZ

    def sweep(k, source, target, e):
        tile_at = [pl.ds(t * LANES, LANES) for t in range(tiles)]
        swapped = [pltpu.roll(source[e, :, at], NZ, 1) for at in tile_at]
        for t, at in enumerate(tile_at):
            v = source[e, :, at]
            new = (1.0 - OMEGA) * v + first[e, :, at]
            new = new + coef[0, e, :, at] * source[e - 1, :, at]
            new = new + coef[1, e, :, at] * source[e + 1, :, at]
            before = swapped[(t - 1) % tiles]
            after = swapped[(t + 1) % tiles]
            new = new + coef[2, e, :, at] * jnp.where(low_half, before, swapped[t])
            new = new + coef[3, e, :, at] * jnp.where(low_half, swapped[t], after)
            new = new + coef[4, e, :, at] * pltpu.roll(v, 1, 1)
            new = new + coef[5, e, :, at] * pltpu.roll(v, LANES - 1, 1)
            target(e, at, new)

    def sweeps(k):
        for n in range(4):
            h_copy(k, n).wait_recv()

        @pl.loop(0, 8)
        def _(e):
            first[e] = coef[6, e] * field[k, e]

        def into(ref):
            def store(e, at, new):
                ref[e, :, at] = new
            return store

        def into_result(e, at, new):
            result[k, e - 3, :, at] = new

        pl.loop(1, 7)(lambda e: sweep(k, first, into(second), e))
        pl.loop(2, 6)(lambda e: sweep(k, second, into(third), e))
        pl.loop(3, 5)(lambda e: sweep(k, third, into_result, e))
        for p in range(2):
            out_copy(k, p, 1).start()

    @pl.loop(0, chunks + 3)
    def _(step):
        @pl.when(step < chunks)
        def _():
            send(step)

        @pl.when((step >= 1) & (step < chunks + 1))
        def _():
            join(step - 1)

        @pl.when((step >= 2) & (step < chunks + 2))
        def _():
            product(step - 2)
            for n in range(4):
                h_copy(step - 2, n).start()

        @pl.when(step >= 3)
        def _():
            sweeps(step - 3)

    @pl.loop(1, nz)
    def _(dz):
        z_copy(dz).wait_send()

    @pl.loop(0, groups)
    def _(g):
        for way in range(3):
            y_copy(g, way).wait_send()
        core_copy(g).wait_send()

    @pl.loop(0, chunks)
    def _(k):
        for slot in range(6):
            x_copy(k, slot).wait_send()
        for n in range(4):
            h_copy(k, n).wait_send()
        for p in range(2):
            for which in range(2):
                out_copy(k, p, which).wait()


def local(bricks, nx, psi_val, psi_cond, dielectric, point_owner, point_cell):
    nb, _, plane = psi_val.shape
    npts = point_owner.shape[0]
    nz = bricks // (CHIPS_Y * CORES)
    groups = min(4, nz)
    fields = npts // nx
    chunks = fields // 8
    rows = bricks * BLOCK

    vmem = pl.BlockSpec(memory_space=pltpu.VMEM)
    dma = pltpu.SemaphoreType.DMA
    hbm = pl.BlockSpec(memory_space=pl.ANY)
    table = pl.pallas_call(
        points_kernel,
        out_shape=jax.ShapeDtypeStruct((8, plane + 2 * LANES), F32),
        in_specs=[vmem, vmem, vmem, hbm, hbm],
        out_specs=vmem,
        scratch_shapes=[pltpu.VMEM((2 * MOST + 1, nb, 2, LANES), BF16), dma((MOST, 2))],
        compiler_params=pltpu.CompilerParams(vmem_limit_bytes=58 << 20),
        name="points",
    )(point_owner.reshape(1, npts), point_cell.reshape(1, npts), dielectric, psi_val, psi_cond)
    pair, potential = pl.pallas_call(
        functools.partial(kernel, nz, nx),
        out_shape=[jax.ShapeDtypeStruct((fields, 2, plane), F32)] * 2,
        in_specs=[
            vmem, hbm, hbm,
        ],
        out_specs=[pl.BlockSpec(memory_space=pl.ANY)] * 2,
        scratch_shapes=[
            pltpu.VMEM((2, nb // 8, 16, plane), BF16),
            pltpu.VMEM((CORES, CHIPS_Y, nz, BLOCK, LANES), BF16),
            pltpu.VMEM((4 * npts, rows), BF16),
            pltpu.VMEM((4 * npts, LANES), F32),
            pltpu.VMEM((nb, 4 * nb), BF16),
            pltpu.VMEM((2, 2 * npts, 2 * nb), BF16),
            pltpu.VMEM((2, 2, npts, plane), F32),
            pltpu.VMEM((6, chunks, 16, plane + LANES), jnp.int16),
            pltpu.VMEM((6, chunks, 16, plane + LANES), jnp.int16),
            pltpu.VMEM((5, 2, plane), F32),
            pltpu.VMEM((16, plane), F32),
            pltpu.VMEM((7, 8, 8, plane), F32),
            pltpu.VMEM((chunks, 8, 8, plane), F32),
            pltpu.VMEM((8, 8, plane), F32),
            pltpu.VMEM((8, 8, plane), F32),
            pltpu.VMEM((8, 8, plane), F32),
            pltpu.VMEM((chunks, 2, 8, plane), F32),
            dma((2, 8)),
            dma((nz,)), dma((nz,)),
            dma((CHIPS_Y, groups)), dma((CHIPS_Y, groups)),
            dma((groups,)), dma((groups,)),
            dma((6, chunks)), dma((6, chunks)),
            dma((chunks, 4)), dma((chunks, 4)),
            dma((4,)), dma((4,)),
            dma((chunks, 2, 2)),
        ],
        compiler_params=pltpu.CompilerParams(
            collective_id=0, has_side_effects=True, vmem_limit_bytes=52 << 20
        ),
        cost_estimate=pl.CostEstimate(
            flops=2 * 2 * 2 * npts * 2 * nb * plane,
            bytes_accessed=8 * nb * plane + 16 * fields * plane,
            transcendentals=0,
        ),
    )(
        table, psi_val.reshape(nb // 8, 8, 2, plane), psi_cond.reshape(nb // 8, 8, 2, plane),
    )
    return pair, potential


def solution(mesh):
    return jax.shard_map(
        functools.partial(local, mesh.shape["brick"], mesh.shape["band"]),
        mesh=mesh,
        in_specs=(P("band", "brick", None), P("band", "brick", None), P("brick", None), P(), P()),
        out_specs=(P("band", "brick", None), P("band", "brick", None)),
        check_vma=False,
    )
```

time: 82.6 us -> 74.3 us (0.90)
  Pallas kernels: 78.7 us -> 70.9 us
    pallas_call x3 -> x2, Pallas kernels: 78.7 us -> 70.9 us  [the longest x1 67.4 us: local(): pl.pallas_call(functools.partial(kernel, nz, nx), out_shape=[jax.ShapeDty...]
    unnamed x12 -> x4, local copies, waits for them, and re-layouts: 3 us -> 2.47 us
where the time goes in v2:
time: 74.3 us; the launch traced here: 74 us
  Pallas kernels  70.9 us (95%)
  local copies, waits for them, and re-layouts  2.47 us (3%)
    pallas_call x1, Pallas kernels, local(): pl.pallas_call(functools.partial(kernel, nz, nx), out_shape=[jax.ShapeDty...  67.4 us
    pallas_call x1, Pallas kernels, local(): pl.pallas_call(points_kernel, out_shape=jax.ShapeDtypeStruct((8, plane +...  3.52 us
    unnamed x4, local copies, waits for them, and re-layouts  2.47 us

profile of v2, /device:TPU:1, one launch (start us, length us, event | category | flops | bytes accessed | tf_op | source)
XLA Modules:
  0.0 74.0 jit_solution(11025366065919795910)
XLA Ops:
  0.6 3.5 %points.1.table_ref = f32[8,2304]{1,0:T(8,128)} custom-call(s32[1,128]{1,0:T(1,128)} %bitcast.6, s32[1,128]{1,0:T(1,128)} %bitcast.7, f32[2,2048]{1,0:T(2,128)} %eps_ref.1, bf16[256,2,2048]{2,1,0:T(2,128)(2,1)} %val_ref.1, bf16[256,2,2048]{2,1,0:T(2,128)(2,1)} %cond_ref.1), custom_call_target="tpu_custom_call" | custom-call | tf_op jit(solution)/shard_map/points/pallas_call | solution.py:507
  4.2 0.0 copy-start
  4.2 0.9 %copy-done = f32[8,2304]{1,0:T(8,128)S(1)} copy-done((f32[8,2304]{1,0:T(8,128)S(1)}, f32[8,2304]{1,0:T(8,128)}, u32[]{:S(2)}) %copy-start) | copy-done | bytes 73752
  5.0 67.4 %shard_map.68 = (f32[32,2,2048]{2,1,0:T(2,128)S(1)}, f32[32,2,2048]{2,1,0:T(2,128)S(1)}) custom-call(f32[8,2304]{1,0:T(8,128)S(1)} %copy-done, bf16[32,8,2,2048]{3,2,1,0:T(2,128)(2,1)} %bitcast.4, bf16[32,8,2,2048]{3,2,1,0:T(2,128)(2,1)} %bitcast.5), custom_call_target="tpu_custom_call" | custom-call | flops 1073741824 | bytes 5242880 | tf_op jit(solution)/shard_map/pallas_call | solution.py:516
  72.5 0.8 %copy.9 = f32[32,2,2048]{2,1,0:T(2,128)} copy(f32[32,2,2048]{2,1,0:T(2,128)S(1)} %get-tuple-element.4) | data formatting | bytes 1048576
  73.3 0.8 %copy.10 = f32[32,2,2048]{2,1,0:T(2,128)} copy(f32[32,2,2048]{2,1,0:T(2,128)S(1)} %get-tuple-element.5) | data formatting | bytes 1048576
Async XLA Ops:
  4.2 0.9 %copy-start = (f32[8,2304]{1,0:T(8,128)S(1)}, f32[8,2304]{1,0:T(8,128)}, u32[]{:S(2)}) copy-start(f32[8,2304]{1,0:T(8,128)} %points.1.table_ref) | copy-start | bytes 221188

commit v3 on v2

v3 whole, which is shorter than its diff:
```python
import functools

import jax
import jax.numpy as jnp
from jax import lax
from jax.experimental import pallas as pl
from jax.experimental.pallas import tpu as pltpu
from jax.sharding import PartitionSpec as P

NZ = 64
FOURPI = 12.566370614359172
OMEGA = 0.8

CORES = 2
CHIPS_Y = 4
MOST = 4
BLOCK = 4 * MOST
GROUP = 512
LANES = 128
STEP = 32700.0
CODE = 128.0
MESH = pl.DeviceIdType.MESH
F32 = jnp.float32
BF16 = jnp.bfloat16


def iota(shape, dim):
    return lax.broadcasted_iota(jnp.int32, shape, dim)


def to(device):
    return dict(device_id=device, device_id_type=MESH)


def kernel(
    nz, nx,
    table_ref, val_ref, cond_ref,
    pair_ref, pot_ref,
    x_buf, g_buf, sel, found, spread, fold, z_buf, part, out_a, in_a, out_c, in_c,
    eps_all, eps_rows, coef, out_h, in_h, field, first, second, third, result,
    load_sem, zs, zr, ys, yr, cs, cr, xas, xar, xcs, xcr, hs, hr, es, er, out_sem,
):
    brick = lax.axis_index("brick")
    band = lax.axis_index("band")
    bricks = nz * CHIPS_Y * CORES
    core = lax.rem(brick, CORES)
    y = lax.rem(brick // CORES, CHIPS_Y)
    z = brick // (CORES * CHIPS_Y)
    nb8, _, _, plane = val_ref.shape
    nb = nb8 * 8
    npts = part.shape[2]
    owners, cells = table_ref[2:3, :npts], table_ref[3:4, :npts]
    fields = npts // nx
    chunks = fields // 8
    groups = min(4, nz)
    per = nz // groups
    tiles = plane // LANES
    parts = plane // GROUP

    def brick_at(zz, yy, cc):
        return (zz * CHIPS_Y + yy) * CORES + cc

    def brick_off(o):
        return lax.rem(brick + o + bricks, bricks)

    def band_off(o):
        return lax.rem(band + o, nx)

    barrier = pltpu.get_barrier_semaphore()

    @pl.loop(1, nz)
    def _(dz):
        pl.semaphore_signal(barrier, 1, **to({"brick": brick_at(lax.rem(z + dz, nz), y, core)}))

    for dy in (1, 3):
        pl.semaphore_signal(
            barrier, 1, **to({"brick": brick_at(z, lax.rem(y + dy, CHIPS_Y), core)})
        )
    pl.semaphore_signal(barrier, 1, **to({"brick": brick_at(z, y, 1 - core)}))
    for dx in (1, 3):
        pl.semaphore_signal(barrier, 1, **to({"band": band_off(dx)}))
    for o in (-2, -1, 1, 2):
        pl.semaphore_signal(barrier, 1, **to({"brick": brick_off(o)}))

    for s, psi in enumerate((val_ref, cond_ref)):
        for i in range(8):
            copy = pltpu.make_async_copy(
                psi.at[:, i], x_buf.at[s, :, 2 * i : 2 * i + 2, :], load_sem.at[s]
            )
            copy.start()

    first_index = iota((npts, npts), 0)
    second_index = iota((npts, npts), 1)
    owner_across = jnp.broadcast_to(owners, (npts, npts))
    owner_down = jnp.sum(
        jnp.where(first_index == second_index, owner_across, 0.0), axis=1, keepdims=True
    )
    same = owner_across == owner_down
    rank_down = jnp.sum(
        jnp.where(same & (second_index < first_index), 1.0, 0.0), axis=1, keepdims=True
    )
    rank_across = jnp.sum(
        jnp.where(same & (first_index < second_index), 1.0, 0.0), axis=0, keepdims=True
    )
    own = owners == brick.astype(F32)
    slot_of = lax.rem(iota((BLOCK, 1), 0), MOST)
    slot_cell = jnp.zeros((BLOCK, 1), F32)
    for j in range(MOST):
        cell = jnp.sum(
            jnp.where(own & (rank_across == j), cells, 0.0),
            axis=1, keepdims=True,
        )
        slot_cell = jnp.where(slot_of == j, cell, slot_cell)
    slot_cell = slot_cell.astype(jnp.int32)
    slot_plane = jnp.where(slot_cell >= plane, 1, 0)
    slot_column = slot_cell - slot_plane * plane
    owner_down = owner_down.astype(jnp.int32)
    away = lax.rem((owner_down >> 3) - z + nz, nz)
    position = jnp.where(away <= nz // 2, 2 * away - 1, 2 * (nz - away))
    position = jnp.where(away == 0, 0, position)
    group_down = jnp.zeros_like(position)
    for g in range(1, groups):
        group_down = group_down + jnp.where(position >= g * per, 1, 0)
    place = ((owner_down & 1) * groups + group_down) * CHIPS_Y + ((owner_down >> 1) & 3)
    place = (place * per + position - group_down * per) * BLOCK + rank_down.astype(jnp.int32)
    pl.semaphore_wait(barrier, nz - 1 + 2 + 1 + 2 + 4)

    for o in (-2, -1, 1, 2):
        copy = pltpu.make_async_remote_copy(
            src_ref=table_ref, dst_ref=eps_all.at[2 - o],
            send_sem=es, recv_sem=er, **to({"brick": brick_off(o)})
        )
        copy.start()

    fold[...] = jnp.where(iota((2 * nb, nb), 0) // 2 == iota((2 * nb, nb), 1), 1.0, 0.0).astype(BF16)

    half = nb // 2
    row = iota((BLOCK, LANES), 0)
    group_row = iota((BLOCK, GROUP), 0)

    taken = jnp.zeros((BLOCK, 2 * nb), F32)
    for s in range(2):
        pltpu.make_async_copy(x_buf.at[s], x_buf.at[s], load_sem.at[s]).wait()

        def take(n, taken):
            start = pl.multiple_of(n * GROUP, GROUP)
            pick = (iota((BLOCK, GROUP), 1) + start == slot_column) & (
                group_row // (2 * MOST) == s
            )
            return taken + lax.dot_general(
                jnp.where(pick, 1.0, 0.0).astype(BF16),
                x_buf[s, :, :, pl.ds(start, GROUP)].reshape(2 * nb, GROUP),
                (((1,), (1,)), ((), ())), preferred_element_type=F32,
            )

        taken = lax.fori_loop(0, parts, take, taken)
    keep = lax.rem(iota((BLOCK, 2 * nb), 1), 2) == slot_plane
    taken = jnp.dot(
        jnp.where(keep, taken, 0.0).astype(BF16), fold[...], preferred_element_type=F32
    )
    mine = jnp.where(lax.rem(row // MOST, 2) == 0, taken[:, :half], taken[:, half:])
    g_buf[core, y, 0] = mine.astype(BF16)

    def z_copy(i):
        away = (i + 1) // 2 if i % 2 else -(i // 2)
        return pltpu.make_async_remote_copy(
            src_ref=g_buf.at[core, y, 0], dst_ref=g_buf.at[core, y, i],
            send_sem=zs, recv_sem=zr.at[i // per],
            **to({"brick": brick_at(lax.rem(z - away + nz, nz), y, core)})
        )

    for i in range(1, nz):
        z_copy(i).start()

    @pl.loop(0, sel.shape[1] // GROUP)
    def _(n):
        column = iota((npts, GROUP), 1) + n * GROUP
        for q in range(4):
            hit = column == place + q * MOST
            sel[pl.ds(q * npts, npts), pl.ds(pl.multiple_of(n * GROUP, GROUP), GROUP)] = (
                jnp.where(hit, 1.0, 0.0).astype(BF16)
            )

    for p in range(2):
        spread[:, 2 * nb * p : 2 * nb * (p + 1)] = jnp.where(
            iota((nb, 2 * nb), 1) == 2 * iota((nb, 2 * nb), 0) + p, 1.0, 0.0
        ).astype(BF16)

    y_up, y_down = lax.rem(y + 1, CHIPS_Y), lax.rem(y + 3, CHIPS_Y)

    def y_copy(g, way):
        odd = g % 2
        source = y if way < 2 else (y_up if odd else y_down)
        target = (y_up, y_down, y_down if odd else y_up)[way]
        part_of = g_buf.at[core, source, pl.ds(g * per, per)]
        return pltpu.make_async_remote_copy(
            src_ref=part_of, dst_ref=part_of, send_sem=ys,
            recv_sem=yr.at[g, 0 if way == odd else 1],
            **to({"brick": brick_at(z, target, core)})
        )

    def y_arrived(g, n):
        block = g_buf.at[core, pl.ds(0, n + 1), pl.ds(g * per, per)]
        pltpu.make_async_remote_copy(
            src_ref=block, dst_ref=block, send_sem=ys, recv_sem=yr.at[g, n],
            **to({"brick": brick_at(z, y_up, core)})
        ).wait_recv()

    def core_copy(g):
        part_of = g_buf.at[core, :, pl.ds(g * per, per)]
        return pltpu.make_async_remote_copy(
            src_ref=part_of, dst_ref=part_of, send_sem=cs, recv_sem=cr.at[g],
            **to({"brick": brick_at(z, y, 1 - core)})
        )

    columns_of = CHIPS_Y * per * BLOCK

    def find(c, g):
        rows = g_buf[c, :, pl.ds(g * per, per)].reshape(columns_of, LANES)
        start = pl.multiple_of((c * groups + g) * columns_of, columns_of)
        return jnp.dot(sel[:, pl.ds(start, columns_of)], rows, preferred_element_type=F32)

    found[...] = jnp.zeros_like(found)
    for step in range(groups + 3):
        if step < groups:
            come = g_buf.at[core, y, pl.ds(max(1, step * per), per if step else per - 1)]
            pltpu.make_async_remote_copy(
                src_ref=come, dst_ref=come, send_sem=zs, recv_sem=zr.at[step],
                **to({"brick": brick_at(lax.rem(z + 1, nz), y, core)})
            ).wait_recv()
            y_copy(step, 0).start()
            y_copy(step, 1).start()
        if 1 <= step <= groups:
            g = step - 1
            y_arrived(g, 0)
            y_copy(g, 2).start()
        if 2 <= step <= groups + 1:
            g = step - 2
            y_arrived(g, 1)
            core_copy(g).start()
            found[...] += find(core, g)
        if step >= 3:
            g = step - 3
            block = g_buf.at[1 - core, :, pl.ds(g * per, per)]
            pltpu.make_async_remote_copy(
                src_ref=block, dst_ref=block, send_sem=cs, recv_sem=cr.at[g],
                **to({"brick": brick_at(z, y, 1 - core)})
            ).wait_recv()
            found[...] += find(1 - core, g)

    for s in range(2):
        at_points = jnp.concatenate(
            [found[(2 * s + i) * npts : (2 * s + i + 1) * npts, :] for i in range(2)], axis=1
        ).astype(BF16)
        wide = jnp.dot(at_points, spread[...], preferred_element_type=F32).astype(BF16)
        for p in range(2):
            z_buf[s, p * npts : (p + 1) * npts, :] = wide[:, 2 * nb * p : 2 * nb * (p + 1)]

    @pl.loop(0, parts)
    def _(n):
        at = pl.ds(pl.multiple_of(n * GROUP, GROUP), GROUP)
        for s in range(2):
            got = jnp.dot(
                z_buf[s], x_buf[s, :, :, at].reshape(2 * nb, GROUP), preferred_element_type=F32
            )
            part[s, :, :, at] = got.reshape(2, npts, GROUP)

    code_lane = iota((16, LANES), 1)

    def pack(values_at, target, count):
        codes = jnp.zeros((16, LANES), F32)
        for n in range(count):
            values = values_at(n)
            most = jnp.max(jnp.abs(values), axis=1, keepdims=True)
            code = jnp.ceil(jnp.log2(jnp.maximum(most, 1e-30)) * CODE)
            codes = jnp.where(code_lane == n, code, codes)
            whole = jnp.round(values * (STEP * jnp.exp2(code * (-1.0 / CODE))))
            target[:, n * GROUP : (n + 1) * GROUP] = whole.astype(jnp.int32).astype(jnp.int16)
        target[:, count * GROUP :] = codes.astype(jnp.int32).astype(jnp.int16)

    def unpacker(source, count):
        codes = source[:, count * GROUP :].astype(jnp.int32).astype(F32)
        scales = jnp.exp2(codes * (1.0 / CODE)) * (1.0 / STEP)

        def values_at(n):
            got = source[:, n * GROUP : (n + 1) * GROUP].astype(jnp.int32).astype(F32)
            return got * scales[:, n : n + 1]

        return values_at

    def held(target, p, k):
        start = pl.multiple_of(target * fields + k * 8, 8)

        def values_at(n):
            at = slice(n * GROUP, (n + 1) * GROUP)
            return jnp.concatenate(
                [part[0, p, pl.ds(start, 8), at], part[1, p, pl.ds(start, 8), at]], axis=0
            )

        return values_at

    up, down, across = band_off(1), band_off(3), band_off(2)
    heading = (up, down)

    def a_copy(k, way):
        return pltpu.make_async_remote_copy(
            src_ref=out_a.at[way, k], dst_ref=in_a.at[way, k],
            send_sem=xas, recv_sem=xar.at[k], **to({"band": heading[way]})
        )

    def c_copy(k, way):
        return pltpu.make_async_remote_copy(
            src_ref=out_c.at[way, k], dst_ref=in_c.at[way, k],
            send_sem=xcs, recv_sem=xcr.at[k], **to({"band": heading[way]})
        )

    def send(k):
        for way in range(2):
            passed, direct = held(across, way, k), held(heading[way], 1 - way, k)
            pack(
                lambda n: passed(n) if n < parts else direct(n - parts),
                out_a.at[way, k], 2 * parts,
            )
            a_copy(k, way).start()

    def join(k):
        both = in_a.at[:, k]
        pltpu.make_async_remote_copy(
            src_ref=both, dst_ref=both, send_sem=xas, recv_sem=xar.at[k], **to({"band": up})
        ).wait_recv()
        for way in range(2):
            mine_at, got_at = held(heading[way], way, k), unpacker(in_a.at[way, k], 2 * parts)
            pack(lambda n: mine_at(n) + got_at(n), out_c.at[way, k], parts)
            c_copy(k, way).start()

    sides = ((-2, 0, 1, 5), (-1, 0, 2, 3), (1, 0, 2, 1), (2, 1, 1, 0))

    def h_copy(k, n):
        o, source, count, target = sides[n]
        return pltpu.make_async_remote_copy(
            src_ref=out_h.at[k, source : source + count],
            dst_ref=in_h.at[k, target : target + count],
            send_sem=hs, recv_sem=hr.at[k], **to({"brick": brick_off(o)})
        )

    def out_copy(which, p, start, count):
        rows = pl.ds(start, count)
        return pltpu.make_async_copy(
            (field, result)[which].at[p, rows], (pair_ref, pot_ref)[which].at[rows, p, :],
            out_sem.at[which],
        )

    def product(k):
        both = in_c.at[:, k]
        pltpu.make_async_remote_copy(
            src_ref=both, dst_ref=both, send_sem=xcs, recv_sem=xcr.at[k], **to({"band": up})
        ).wait_recv()
        rows = pl.ds(pl.multiple_of(k * 8, 8), 8)
        for p in range(2):
            direct = unpacker(in_a.at[1 - p, k], 2 * parts)
            parts_at = (
                held(band, p, k), lambda n: direct(n + parts), unpacker(in_c.at[p, k], parts)
            )
            for n in range(parts):
                total = sum(values_at(n) for values_at in parts_at)
                pair = total[:8, :] * total[8:, :]
                field[p, rows, n * GROUP : (n + 1) * GROUP] = pair

            def halves(n):
                return jnp.concatenate(
                    [
                        field[p, rows, m * GROUP : (m + 1) * GROUP]
                        for m in (n, n + parts // 2)
                    ],
                    axis=0,
                )

            pack(halves, out_h.at[k, p], parts // 2)

        @pl.when(k == chunks - 1)
        def _():
            for p in range(2):
                out_copy(0, p, 0, fields).start()

    low_half = iota((8, LANES), 1) < NZ

    def sweep(k, source, target, e):
        tile_at = [pl.ds(t * LANES, LANES) for t in range(tiles)]
        swapped = [pltpu.roll(source[e, :, at], NZ, 1) for at in tile_at]
        for t, at in enumerate(tile_at):
            v = source[e, :, at]
            new = (1.0 - OMEGA) * v + first[e, :, at]
            new = new + coef[0, e, :, at] * source[e - 1, :, at]
            new = new + coef[1, e, :, at] * source[e + 1, :, at]
            before = swapped[(t - 1) % tiles]
            after = swapped[(t + 1) % tiles]
            new = new + coef[2, e, :, at] * jnp.where(low_half, before, swapped[t])
            new = new + coef[3, e, :, at] * jnp.where(low_half, swapped[t], after)
            new = new + coef[4, e, :, at] * pltpu.roll(v, 1, 1)
            new = new + coef[5, e, :, at] * pltpu.roll(v, LANES - 1, 1)
            target(e, at, new)

    def sweeps(k):
        come = in_h.at[k]
        pltpu.make_async_remote_copy(
            src_ref=come, dst_ref=come, send_sem=hs, recv_sem=hr.at[k],
            **to({"brick": brick_off(1)})
        ).wait_recv()
        rows = pl.ds(pl.multiple_of(k * 8, 8), 8)
        for p in range(2):
            first[3 + p] = coef[6, 3 + p] * field[p, rows, :]

        @pl.loop(0, 6)
        def _(i):
            e = i + 2 * (i // 3)
            halves = unpacker(in_h.at[k, i], parts // 2)
            for n in range(parts // 2):
                values = halves(n)
                for m in range(2):
                    at = slice((n + m * parts // 2) * GROUP, (n + m * parts // 2 + 1) * GROUP)
                    first[e, :, at] = coef[6, e, :, at] * values[8 * m : 8 * m + 8, :]

        def into(ref):
            def store(e, at, new):
                ref[e, :, at] = new
            return store

        def into_result(e, at, new):
            result[e - 3, rows, at] = new

        pl.loop(1, 7)(lambda e: sweep(k, first, into(second), e))
        pl.loop(2, 6)(lambda e: sweep(k, second, into(third), e))
        pl.loop(3, 5)(lambda e: sweep(k, third, into_result, e))
        last = 8 * (chunks - 1)

        @pl.when(k == chunks - 2)
        def _():
            for p in range(2):
                out_copy(1, p, 0, last).start()

        @pl.when(k == chunks - 1)
        def _():
            for p in range(2):
                out_copy(1, p, last, 8).start()

    def coefficients():
        pltpu.make_async_remote_copy(
            src_ref=eps_all.at[0:4], dst_ref=eps_all.at[0:4], send_sem=es, recv_sem=er,
            **to({"brick": brick_off(1)})
        ).wait()
        for o in range(5):
            eps_rows[2 * o : 2 * o + 2, :] = table_ref[:2, :] if o == 2 else eps_all[o, :2, :]
        here = eps_rows[1:9, :]
        xminus = 0.5 * (here + eps_rows[0:8, :])
        xplus = 0.5 * (here + eps_rows[2:10, :])
        depth = lax.rem(iota((8, plane), 1), NZ)
        above = depth < NZ - 1
        below = depth > 0
        yplus = 0.5 * (here + pltpu.roll(here, plane - NZ, 1))
        yminus = 0.5 * (here + pltpu.roll(here, NZ, 1))
        zplus = 0.5 * (here + jnp.where(above, pltpu.roll(here, plane - 1, 1), here))
        zminus = 0.5 * (here + jnp.where(below, pltpu.roll(here, 1, 1), here))
        scale = OMEGA / (xplus + xminus + yplus + yminus + zplus + zminus)
        faces = (
            xminus, xplus, yminus, yplus,
            jnp.where(below, zminus, 0.0), jnp.where(above, zplus, 0.0), FOURPI,
        )
        for n, face in enumerate(faces):
            scaled = scale * face
            for e in range(8):
                coef[n, e] = jnp.broadcast_to(scaled[e : e + 1, :], (8, plane))

    @pl.loop(0, chunks + 3)
    def _(step):
        @pl.when(step < chunks)
        def _():
            send(step)

        @pl.when((step >= 1) & (step < chunks + 1))
        def _():
            join(step - 1)

        @pl.when(step == 2)
        def _():
            coefficients()

        @pl.when((step >= 2) & (step < chunks + 2))
        def _():
            product(step - 2)
            for n in range(4):
                h_copy(step - 2, n).start()

        @pl.when(step >= 3)
        def _():
            sweeps(step - 3)

    def sent(ref, sem, recv_sem):
        pltpu.make_async_remote_copy(
            src_ref=ref, dst_ref=ref, send_sem=sem, recv_sem=recv_sem,
            **to({"brick": brick_off(1)})
        ).wait_send()

    sent(g_buf.at[core, y, pl.ds(1, nz - 1)], zs, zr.at[0])
    sent(g_buf.at[core, pl.ds(0, 3)], ys, yr.at[0, 0])
    sent(g_buf.at[core], cs, cr.at[0])
    sent(out_a, xas, xar.at[0])
    sent(out_c, xcs, xcr.at[0])
    sent(in_h, hs, hr.at[0])
    for which, ref in enumerate((field, result)):
        pltpu.make_async_copy(ref, ref, out_sem.at[which]).wait()


def local(bricks, nx, psi_val, psi_cond, dielectric, point_owner, point_cell):
    nb, _, plane = psi_val.shape
    npts = point_owner.shape[0]
    nz = bricks // (CHIPS_Y * CORES)
    groups = min(4, nz)
    fields = npts // nx
    chunks = fields // 8
    rows = bricks * BLOCK

    def row(values):
        return jnp.pad(values[None, :], ((0, 0), (0, plane - npts))).astype(F32)

    table = jnp.concatenate([dielectric, row(point_owner), row(point_cell)], axis=0)

    vmem = pl.BlockSpec(memory_space=pltpu.VMEM)
    dma = pltpu.SemaphoreType.DMA
    pair, potential = pl.pallas_call(
        functools.partial(kernel, nz, nx),
        out_shape=[jax.ShapeDtypeStruct((fields, 2, plane), F32)] * 2,
        in_specs=[
            vmem, pl.BlockSpec(memory_space=pl.ANY), pl.BlockSpec(memory_space=pl.ANY),
        ],
        out_specs=[pl.BlockSpec(memory_space=pl.ANY)] * 2,
        scratch_shapes=[
            pltpu.VMEM((2, nb // 8, 16, plane), BF16),
            pltpu.VMEM((CORES, CHIPS_Y, nz, BLOCK, LANES), BF16),
            pltpu.VMEM((4 * npts, rows), BF16),
            pltpu.VMEM((4 * npts, LANES), F32),
            pltpu.VMEM((nb, 4 * nb), BF16),
            pltpu.VMEM((2 * nb, nb), BF16),
            pltpu.VMEM((2, 2 * npts, 2 * nb), BF16),
            pltpu.VMEM((2, 2, npts, plane), F32),
            pltpu.VMEM((2, chunks, 16, 2 * plane + LANES), jnp.int16),
            pltpu.VMEM((2, chunks, 16, 2 * plane + LANES), jnp.int16),
            pltpu.VMEM((2, chunks, 16, plane + LANES), jnp.int16),
            pltpu.VMEM((2, chunks, 16, plane + LANES), jnp.int16),
            pltpu.VMEM((5, 4, plane), F32),
            pltpu.VMEM((16, plane), F32),
            pltpu.VMEM((7, 8, 8, plane), F32),
            pltpu.VMEM((chunks, 2, 16, plane // 2 + LANES), jnp.int16),
            pltpu.VMEM((chunks, 6, 16, plane // 2 + LANES), jnp.int16),
            pltpu.VMEM((2, fields, plane), F32),
            pltpu.VMEM((8, 8, plane), F32),
            pltpu.VMEM((8, 8, plane), F32),
            pltpu.VMEM((8, 8, plane), F32),
            pltpu.VMEM((2, fields, plane), F32),
            dma((2,)),
            dma, dma((groups,)),
            dma, dma((groups, 2)),
            dma, dma((groups,)),
            dma, dma((chunks,)),
            dma, dma((chunks,)),
            dma, dma((chunks,)),
            dma, dma,
            dma((2,)),
        ],
        compiler_params=pltpu.CompilerParams(
            collective_id=0, has_side_effects=True, vmem_limit_bytes=52 << 20
        ),
        cost_estimate=pl.CostEstimate(
            flops=2 * 2 * 2 * npts * 2 * nb * plane,
            bytes_accessed=8 * nb * plane + 16 * fields * plane,
            transcendentals=0,
        ),
    )(
        table, psi_val.reshape(nb // 8, 8, 2, plane), psi_cond.reshape(nb // 8, 8, 2, plane),
    )
    return pair, potential


def solution(mesh):
    return jax.shard_map(
        functools.partial(local, mesh.shape["brick"], mesh.shape["band"]),
        mesh=mesh,
        in_specs=(P("band", "brick", None), P("band", "brick", None), P("brick", None), P(), P()),
        out_specs=(P("band", "brick", None), P("band", "brick", None)),
        check_vma=False,
    )
```

time: 74.3 us -> 72.4 us (0.974)
  Pallas kernels: 70.9 us -> 68.6 us
  other arithmetic: 0 us -> 1.43 us
  local copies, waits for them, and re-layouts: 2.47 us -> 1.59 us
    pallas_call x1 -> x0, Pallas kernels: 3.52 us -> none  [local(): pl.pallas_call(points_kernel, out_shape=jax.ShapeDtypeStruct((8, plane +...]
    pallas_call x1, Pallas kernels: 67.4 us -> 68.6 us  [local(): pl.pallas_call(functools.partial(kernel, nz, nx), out_shape=[jax.ShapeDty...]
    unnamed x4 -> x2, local copies, waits for them, and re-layouts: 2.47 us -> 1.59 us
    concatenate x0 -> x1, other arithmetic: none -> 0.75 us  [local(): jnp.concatenate([dielectric, row(point_owner), row(point_cell)], axis=0)]
where the time goes in v3:
time: 72.4 us; the launch traced here: 72.2 us
  Pallas kernels  68.6 us (95%)
  local copies, waits for them, and re-layouts  1.59 us (2%)
  other arithmetic  1.43 us (2%)
    pallas_call x1, Pallas kernels, local(): pl.pallas_call(functools.partial(kernel, nz, nx), out_shape=[jax.ShapeDty...  68.6 us
    unnamed x2, local copies, waits for them, and re-layouts  1.59 us

profile of v3, /device:TPU:1, one launch (start us, length us, event | category | flops | bytes accessed | tf_op | source)
XLA Modules:
  0.0 72.2 jit_solution(6940464717107482838)
XLA Ops:
  0.6 0.7 pad_convert_fusion
  1.3 0.7 %pad_maximum_fusion.table_ref = f32[4,2048]{1,0:T(4,128)S(1)} fusion(f32[1,2048]{1,0:T(1,128)S(1)} %get-tuple-element.2, f32[1,2048]{1,0:T(1,128)S(1)} %get-tuple-element.3, f32[2,2048]{1,0:T(2,128)} %param.7), kind=kLoop, calls=%fused_computation | loop fusion | flops 16384 | bytes 65536 | tf_op jit(solution)/shard_map/concatenate | solution.py:525
  2.1 68.6 %shard_map.68 = (f32[32,2,2048]{2,1,0:T(2,128)S(1)}, f32[32,2,2048]{2,1,0:T(2,128)S(1)}) custom-call(f32[4,2048]{1,0:T(4,128)S(1)} %pad_maximum_fusion.table_ref, bf16[32,8,2,2048]{3,2,1,0:T(2,128)(2,1)} %bitcast.4, bf16[32,8,2,2048]{3,2,1,0:T(2,128)(2,1)} %bitcast.5), custom_call_target="tpu_custom_call" | custom-call | flops 1073741824 | bytes 5242880 | tf_op jit(solution)/shard_map/pallas_call | solution.py:529
  70.6 0.8 %copy.9 = f32[32,2,2048]{2,1,0:T(2,128)} copy(f32[32,2,2048]{2,1,0:T(2,128)S(1)} %get-tuple-element.6) | data formatting | bytes 1048576
  71.4 0.8 %copy.10 = f32[32,2,2048]{2,1,0:T(2,128)} copy(f32[32,2,2048]{2,1,0:T(2,128)S(1)} %get-tuple-element.7) | data formatting | bytes 1048576

commit v4 on v3

--- a/solution.py
+++ b/solution.py
@@ -103,7 +103,7 @@
         jnp.where(same & (first_index < second_index), 1.0, 0.0), axis=0, keepdims=True
     )
     own = owners == brick.astype(F32)
-    slot_of = lax.rem(iota((BLOCK, 1), 0), MOST)
+    slot_of = iota((BLOCK, 1), 0) & (MOST - 1)
     slot_cell = jnp.zeros((BLOCK, 1), F32)
     for j in range(MOST):
         cell = jnp.sum(
@@ -115,7 +115,8 @@
     slot_plane = jnp.where(slot_cell >= plane, 1, 0)
     slot_column = slot_cell - slot_plane * plane
     owner_down = owner_down.astype(jnp.int32)
-    away = lax.rem((owner_down >> 3) - z + nz, nz)
+    away = (owner_down >> 3) - z
+    away = jnp.where(away < 0, away + nz, away)
     position = jnp.where(away <= nz // 2, 2 * away - 1, 2 * (nz - away))
     position = jnp.where(away == 0, 0, position)
     group_down = jnp.zeros_like(position)
@@ -132,7 +133,7 @@
         )
         copy.start()
 
-    fold[...] = jnp.where(iota((2 * nb, nb), 0) // 2 == iota((2 * nb, nb), 1), 1.0, 0.0).astype(BF16)
+    fold[...] = jnp.where((iota((2 * nb, nb), 0) >> 1) == iota((2 * nb, nb), 1), 1.0, 0.0).astype(BF16)
 
     half = nb // 2
     row = iota((BLOCK, LANES), 0)
@@ -145,7 +146,7 @@
         def take(n, taken):
             start = pl.multiple_of(n * GROUP, GROUP)
             pick = (iota((BLOCK, GROUP), 1) + start == slot_column) & (
-                group_row // (2 * MOST) == s
+                (group_row >> 3) == s
             )
             return taken + lax.dot_general(
                 jnp.where(pick, 1.0, 0.0).astype(BF16),
@@ -154,11 +155,11 @@
             )
 
         taken = lax.fori_loop(0, parts, take, taken)
-    keep = lax.rem(iota((BLOCK, 2 * nb), 1), 2) == slot_plane
+    keep = (iota((BLOCK, 2 * nb), 1) & 1) == slot_plane
     taken = jnp.dot(
         jnp.where(keep, taken, 0.0).astype(BF16), fold[...], preferred_element_type=F32
     )
-    mine = jnp.where(lax.rem(row // MOST, 2) == 0, taken[:, :half], taken[:, half:])
+    mine = jnp.where(((row >> 2) & 1) == 0, taken[:, :half], taken[:, half:])
     g_buf[core, y, 0] = mine.astype(BF16)
 
     def z_copy(i):
@@ -267,16 +268,20 @@
 
     code_lane = iota((16, LANES), 1)
 
-    def pack(values_at, target, count):
-        codes = jnp.zeros((16, LANES), F32)
-        for n in range(count):
-            values = values_at(n)
-            most = jnp.max(jnp.abs(values), axis=1, keepdims=True)
+    def pack(*messages):
+        scales = []
+        for values_at, target, count in messages:
+            most = jnp.zeros((16, LANES), F32)
+            for n in range(count):
+                peak = jnp.max(jnp.abs(values_at(n)), axis=1, keepdims=True)
+                most = jnp.where(code_lane == n, peak, most)
             code = jnp.ceil(jnp.log2(jnp.maximum(most, 1e-30)) * CODE)
-            codes = jnp.where(code_lane == n, code, codes)
-            whole = jnp.round(values * (STEP * jnp.exp2(code * (-1.0 / CODE))))
-            target[:, n * GROUP : (n + 1) * GROUP] = whole.astype(jnp.int32).astype(jnp.int16)
-        target[:, count * GROUP :] = codes.astype(jnp.int32).astype(jnp.int16)
+            scales.append((code, STEP * jnp.exp2(code * (-1.0 / CODE))))
+        for (values_at, target, count), (code, scale) in zip(messages, scales):
+            target[:, count * GROUP :] = code.astype(jnp.int32).astype(jnp.int16)
+            for n in range(count):
+                whole = jnp.round(values_at(n) * scale[:, n : n + 1])
+                target[:, n * GROUP : (n + 1) * GROUP] = whole.astype(jnp.int32).astype(jnp.int16)
 
     def unpacker(source, count):
         codes = source[:, count * GROUP :].astype(jnp.int32).astype(F32)
@@ -315,12 +320,15 @@
         )
 
     def send(k):
-        for way in range(2):
+        def message(way):
             passed, direct = held(across, way, k), held(heading[way], 1 - way, k)
-            pack(
+            return (
                 lambda n: passed(n) if n < parts else direct(n - parts),
                 out_a.at[way, k], 2 * parts,
             )
+
+        pack(message(0), message(1))
+        for way in range(2):
             a_copy(k, way).start()
 
     def join(k):
@@ -328,9 +336,12 @@
         pltpu.make_async_remote_copy(
             src_ref=both, dst_ref=both, send_sem=xas, recv_sem=xar.at[k], **to({"band": up})
         ).wait_recv()
+        def message(way):
+            mine_at, got_at = held(heading[way], way, k), unpacker(in_a.at[way, k], 2 * parts)
+            return lambda n: mine_at(n) + got_at(n), out_c.at[way, k], parts
+
+        pack(message(0), message(1))
         for way in range(2):
-            mine_at, got_at = held(heading[way], way, k), unpacker(in_a.at[way, k], 2 * parts)
-            pack(lambda n: mine_at(n) + got_at(n), out_c.at[way, k], parts)
             c_copy(k, way).start()
 
     sides = ((-2, 0, 1, 5), (-1, 0, 2, 3), (1, 0, 2, 1), (2, 1, 1, 0))
@@ -361,11 +372,14 @@
             parts_at = (
                 held(band, p, k), lambda n: direct(n + parts), unpacker(in_c.at[p, k], parts)
             )
+            pairs = []
             for n in range(parts):
                 total = sum(values_at(n) for values_at in parts_at)
-                pair = total[:8, :] * total[8:, :]
-                field[p, rows, n * GROUP : (n + 1) * GROUP] = pair
-
+                pairs.append(total[:8, :] * total[8:, :])
+            for n in range(parts):
+                field[p, rows, n * GROUP : (n + 1) * GROUP] = pairs[n]
+
+        def message(p):
             def halves(n):
                 return jnp.concatenate(
                     [
@@ -375,7 +389,9 @@
                     axis=0,
                 )
 
-            pack(halves, out_h.at[k, p], parts // 2)
+            return halves, out_h.at[k, p], parts // 2
+
+        pack(message(0), message(1))
 
         @pl.when(k == chunks - 1)
         def _():
@@ -384,21 +400,23 @@
 
     low_half = iota((8, LANES), 1) < NZ
 
-    def sweep(k, source, target, e):
+    def sweep(source, e):
         tile_at = [pl.ds(t * LANES, LANES) for t in range(tiles)]
         swapped = [pltpu.roll(source[e, :, at], NZ, 1) for at in tile_at]
+        news = []
         for t, at in enumerate(tile_at):
             v = source[e, :, at]
-            new = (1.0 - OMEGA) * v + first[e, :, at]
-            new = new + coef[0, e, :, at] * source[e - 1, :, at]
-            new = new + coef[1, e, :, at] * source[e + 1, :, at]
             before = swapped[(t - 1) % tiles]
             after = swapped[(t + 1) % tiles]
-            new = new + coef[2, e, :, at] * jnp.where(low_half, before, swapped[t])
-            new = new + coef[3, e, :, at] * jnp.where(low_half, swapped[t], after)
-            new = new + coef[4, e, :, at] * pltpu.roll(v, 1, 1)
-            new = new + coef[5, e, :, at] * pltpu.roll(v, LANES - 1, 1)
-            target(e, at, new)
+            alone = (1.0 - OMEGA) * v + first[e, :, at]
+            along_x = coef[0, e, :, at] * source[e - 1, :, at]
+            along_x = along_x + coef[1, e, :, at] * source[e + 1, :, at]
+            along_y = coef[2, e, :, at] * jnp.where(low_half, before, swapped[t])
+            along_y = along_y + coef[3, e, :, at] * jnp.where(low_half, swapped[t], after)
+            along_z = coef[4, e, :, at] * pltpu.roll(v, 1, 1)
+            along_z = along_z + coef[5, e, :, at] * pltpu.roll(v, LANES - 1, 1)
+            news.append((alone + along_x) + (along_y + along_z))
+        return zip(tile_at, news)
 
     def sweeps(k):
         come = in_h.at[k]
@@ -414,23 +432,27 @@
         def _(i):
             e = i + 2 * (i // 3)
             halves = unpacker(in_h.at[k, i], parts // 2)
-            for n in range(parts // 2):
-                values = halves(n)
-                for m in range(2):
-                    at = slice((n + m * parts // 2) * GROUP, (n + m * parts // 2 + 1) * GROUP)
-                    first[e, :, at] = coef[6, e, :, at] * values[8 * m : 8 * m + 8, :]
-
-        def into(ref):
-            def store(e, at, new):
-                ref[e, :, at] = new
-            return store
-
-        def into_result(e, at, new):
-            result[e - 3, rows, at] = new
-
-        pl.loop(1, 7)(lambda e: sweep(k, first, into(second), e))
-        pl.loop(2, 6)(lambda e: sweep(k, second, into(third), e))
-        pl.loop(3, 5)(lambda e: sweep(k, third, into_result, e))
+            values = [halves(n) for n in range(parts // 2)]
+            for m in range(parts):
+                at = slice(m * GROUP, (m + 1) * GROUP)
+                half = values[m % (parts // 2)][8 * (m // (parts // 2)) :, :][:8, :]
+                first[e, :, at] = coef[6, e, :, at] * half
+
+        @pl.loop(1, 7)
+        def _(e):
+            for at, new in sweep(first, e):
+                second[e, :, at] = new
+
+        @pl.loop(2, 6)
+        def _(e):
+            for at, new in sweep(second, e):
+                third[e, :, at] = new
+
+        @pl.loop(3, 5)
+        def _(e):
+            for at, new in sweep(third, e):
+                result[e - 3, rows, at] = new
+
         last = 8 * (chunks - 1)
 
         @pl.when(k == chunks - 2)
@@ -453,7 +475,7 @@
         here = eps_rows[1:9, :]
         xminus = 0.5 * (here + eps_rows[0:8, :])
         xplus = 0.5 * (here + eps_rows[2:10, :])
-        depth = lax.rem(iota((8, plane), 1), NZ)
+        depth = iota((8, plane), 1) & (NZ - 1)
         above = depth < NZ - 1
         below = depth > 0
         yplus = 0.5 * (here + pltpu.roll(here, plane - NZ, 1))

time: 72.4 us -> 72.8 us (level)
  no operation moved by 1% of the time
where the time goes in v4:
time: 72.8 us; the launch traced here: 72.6 us
  Pallas kernels  68.9 us (95%)
  local copies, waits for them, and re-layouts  1.59 us (2%)
  other arithmetic  1.43 us (2%)
    pallas_call x1, Pallas kernels, local(): pl.pallas_call(functools.partial(kernel, nz, nx), out_shape=[jax.ShapeDty...  68.9 us
    unnamed x2, local copies, waits for them, and re-layouts  1.59 us

profile of v4, /device:TPU:1, one launch (start us, length us, event | category | flops | bytes accessed | tf_op | source)
XLA Modules:
  0.0 72.6 jit_solution(5517188055591602077)
XLA Ops:
  0.6 0.7 pad_convert_fusion
  1.3 0.7 %pad_maximum_fusion.table_ref = f32[4,2048]{1,0:T(4,128)S(1)} fusion(f32[1,2048]{1,0:T(1,128)S(1)} %get-tuple-element.2, f32[1,2048]{1,0:T(1,128)S(1)} %get-tuple-element.3, f32[2,2048]{1,0:T(2,128)} %param.7), kind=kLoop, calls=%fused_computation | loop fusion | flops 16384 | bytes 65536 | tf_op jit(solution)/shard_map/concatenate | solution.py:547
  2.1 68.9 %shard_map.68 = (f32[32,2,2048]{2,1,0:T(2,128)S(1)}, f32[32,2,2048]{2,1,0:T(2,128)S(1)}) custom-call(f32[4,2048]{1,0:T(4,128)S(1)} %pad_maximum_fusion.table_ref, bf16[32,8,2,2048]{3,2,1,0:T(2,128)(2,1)} %bitcast.4, bf16[32,8,2,2048]{3,2,1,0:T(2,128)(2,1)} %bitcast.5), custom_call_target="tpu_custom_call" | custom-call | flops 1073741824 | bytes 5242880 | tf_op jit(solution)/shard_map/pallas_call | solution.py:551
  71.0 0.8 %copy.9 = f32[32,2,2048]{2,1,0:T(2,128)} copy(f32[32,2,2048]{2,1,0:T(2,128)S(1)} %get-tuple-element.6) | data formatting | bytes 1048576
  71.8 0.8 %copy.10 = f32[32,2,2048]{2,1,0:T(2,128)} copy(f32[32,2,2048]{2,1,0:T(2,128)S(1)} %get-tuple-element.7) | data formatting | bytes 1048576

commit v5 on v4

--- a/solution.py
+++ b/solution.py
@@ -268,6 +268,9 @@
 
     code_lane = iota((16, LANES), 1)
 
+    def lanes_of(n):
+        return slice(n * GROUP + LANES * (n >= parts), (n + 1) * GROUP + LANES * (n >= parts))
+
     def pack(*messages):
         scales = []
         for values_at, target, count in messages:
@@ -278,17 +281,19 @@
             code = jnp.ceil(jnp.log2(jnp.maximum(most, 1e-30)) * CODE)
             scales.append((code, STEP * jnp.exp2(code * (-1.0 / CODE))))
         for (values_at, target, count), (code, scale) in zip(messages, scales):
-            target[:, count * GROUP :] = code.astype(jnp.int32).astype(jnp.int16)
+            first_of = min(count, parts) * GROUP
+            target[:, first_of : first_of + LANES] = code.astype(jnp.int32).astype(jnp.int16)
             for n in range(count):
                 whole = jnp.round(values_at(n) * scale[:, n : n + 1])
-                target[:, n * GROUP : (n + 1) * GROUP] = whole.astype(jnp.int32).astype(jnp.int16)
+                target[:, lanes_of(n)] = whole.astype(jnp.int32).astype(jnp.int16)
 
     def unpacker(source, count):
-        codes = source[:, count * GROUP :].astype(jnp.int32).astype(F32)
+        first_of = min(count, parts) * GROUP
+        codes = source[:, first_of : first_of + LANES].astype(jnp.int32).astype(F32)
         scales = jnp.exp2(codes * (1.0 / CODE)) * (1.0 / STEP)
 
         def values_at(n):
-            got = source[:, n * GROUP : (n + 1) * GROUP].astype(jnp.int32).astype(F32)
+            got = source[:, lanes_of(n)].astype(jnp.int32).astype(F32)
             return got * scales[:, n : n + 1]
 
         return values_at
@@ -307,10 +312,13 @@
     up, down, across = band_off(1), band_off(3), band_off(2)
     heading = (up, down)
 
-    def a_copy(k, way):
+    pieces = ((0, plane + LANES), (plane + LANES, plane))
+
+    def a_copy(k, way, piece):
+        at = pl.ds(*pieces[piece])
         return pltpu.make_async_remote_copy(
-            src_ref=out_a.at[way, k], dst_ref=in_a.at[way, k],
-            send_sem=xas, recv_sem=xar.at[k], **to({"band": heading[way]})
+            src_ref=out_a.at[way, k, :, at], dst_ref=in_a.at[way, k, :, at],
+            send_sem=xas, recv_sem=xar.at[piece, k], **to({"band": heading[way]})
         )
 
     def c_copy(k, way):
@@ -328,14 +336,19 @@
             )
 
         pack(message(0), message(1))
-        for way in range(2):
-            a_copy(k, way).start()
+        for piece in range(2):
+            for way in range(2):
+                a_copy(k, way, piece).start()
+
+    def arrived(k, piece):
+        both = in_a.at[:, k, :, pl.ds(*pieces[piece])]
+        pltpu.make_async_remote_copy(
+            src_ref=both, dst_ref=both, send_sem=xas, recv_sem=xar.at[piece, k],
+            **to({"band": up})
+        ).wait_recv()
 
     def join(k):
-        both = in_a.at[:, k]
-        pltpu.make_async_remote_copy(
-            src_ref=both, dst_ref=both, send_sem=xas, recv_sem=xar.at[k], **to({"band": up})
-        ).wait_recv()
+        arrived(k, 0)
         def message(way):
             mine_at, got_at = held(heading[way], way, k), unpacker(in_a.at[way, k], 2 * parts)
             return lambda n: mine_at(n) + got_at(n), out_c.at[way, k], parts
@@ -362,6 +375,7 @@
         )
 
     def product(k):
+        arrived(k, 1)
         both = in_c.at[:, k]
         pltpu.make_async_remote_copy(
             src_ref=both, dst_ref=both, send_sem=xcs, recv_sem=xcr.at[k], **to({"band": up})
@@ -492,29 +506,29 @@
             for e in range(8):
                 coef[n, e] = jnp.broadcast_to(scaled[e : e + 1, :], (8, plane))
 
-    @pl.loop(0, chunks + 3)
+    @pl.loop(0, chunks + 6)
     def _(step):
         @pl.when(step < chunks)
         def _():
             send(step)
 
-        @pl.when((step >= 1) & (step < chunks + 1))
-        def _():
-            join(step - 1)
-
-        @pl.when(step == 2)
+        @pl.when((step >= 2) & (step < chunks + 2))
+        def _():
+            join(step - 2)
+
+        @pl.when(step == 3)
         def _():
             coefficients()
 
-        @pl.when((step >= 2) & (step < chunks + 2))
-        def _():
-            product(step - 2)
+        @pl.when((step >= 4) & (step < chunks + 4))
+        def _():
+            product(step - 4)
             for n in range(4):
-                h_copy(step - 2, n).start()
-
-        @pl.when(step >= 3)
-        def _():
-            sweeps(step - 3)
+                h_copy(step - 4, n).start()
+
+        @pl.when(step >= 6)
+        def _():
+            sweeps(step - 6)
 
     def sent(ref, sem, recv_sem):
         pltpu.make_async_remote_copy(
@@ -525,7 +539,7 @@
     sent(g_buf.at[core, y, pl.ds(1, nz - 1)], zs, zr.at[0])
     sent(g_buf.at[core, pl.ds(0, 3)], ys, yr.at[0, 0])
     sent(g_buf.at[core], cs, cr.at[0])
-    sent(out_a, xas, xar.at[0])
+    sent(out_a, xas, xar.at[0, 0])
     sent(out_c, xcs, xcr.at[0])
     sent(in_h, hs, hr.at[0])
     for which, ref in enumerate((field, result)):
@@ -582,7 +596,7 @@
             dma, dma((groups,)),
             dma, dma((groups, 2)),
             dma, dma((groups,)),
-            dma, dma((chunks,)),
+            dma, dma((2, chunks)),
             dma, dma((chunks,)),
             dma, dma((chunks,)),
             dma, dma,

time: 72.8 us -> 73.7 us (1.012)
  Pallas kernels: 68.9 us -> 69.9 us
    pallas_call x1, Pallas kernels: 68.9 us -> 69.9 us  [local(): pl.pallas_call(functools.partial(kernel, nz, nx), out_shape=[jax.ShapeDty...]
where the time goes in v5:
time: 73.7 us; the launch traced here: 73.5 us
  Pallas kernels  69.9 us (95%)
  local copies, waits for them, and re-layouts  1.59 us (2%)
  other arithmetic  1.43 us (2%)
    pallas_call x1, Pallas kernels, local(): pl.pallas_call(functools.partial(kernel, nz, nx), out_shape=[jax.ShapeDty...  69.9 us
    unnamed x2, local copies, waits for them, and re-layouts  1.59 us

profile of v5, /device:TPU:1, one launch (start us, length us, event | category | flops | bytes accessed | tf_op | source)
XLA Modules:
  0.0 73.5 jit_solution(4574230445174567712)
XLA Ops:
  0.6 0.7 pad_convert_fusion
  1.3 0.7 %pad_maximum_fusion.table_ref = f32[4,2048]{1,0:T(4,128)S(1)} fusion(f32[1,2048]{1,0:T(1,128)S(1)} %get-tuple-element.2, f32[1,2048]{1,0:T(1,128)S(1)} %get-tuple-element.3, f32[2,2048]{1,0:T(2,128)} %param.7), kind=kLoop, calls=%fused_computation | loop fusion | flops 16384 | bytes 65536 | tf_op jit(solution)/shard_map/concatenate | solution.py:561
  2.1 69.9 %shard_map.68 = (f32[32,2,2048]{2,1,0:T(2,128)S(1)}, f32[32,2,2048]{2,1,0:T(2,128)S(1)}) custom-call(f32[4,2048]{1,0:T(4,128)S(1)} %pad_maximum_fusion.table_ref, bf16[32,8,2,2048]{3,2,1,0:T(2,128)(2,1)} %bitcast.4, bf16[32,8,2,2048]{3,2,1,0:T(2,128)(2,1)} %bitcast.5), custom_call_target="tpu_custom_call" | custom-call | flops 1073741824 | bytes 5242880 | tf_op jit(solution)/shard_map/pallas_call | solution.py:565
  71.9 0.8 %copy.9 = f32[32,2,2048]{2,1,0:T(2,128)} copy(f32[32,2,2048]{2,1,0:T(2,128)S(1)} %get-tuple-element.6) | data formatting | bytes 1048576
  72.7 0.8 %copy.10 = f32[32,2,2048]{2,1,0:T(2,128)} copy(f32[32,2,2048]{2,1,0:T(2,128)S(1)} %get-tuple-element.7) | data formatting | bytes 1048576

commit v6 on v5

--- a/solution.py
+++ b/solution.py
@@ -36,7 +36,7 @@
     nz, nx,
     table_ref, val_ref, cond_ref,
     pair_ref, pot_ref,
-    x_buf, g_buf, sel, found, spread, fold, z_buf, part, out_a, in_a, out_c, in_c,
+    x_buf, g_buf, sel, found, spread, fold, pick, taken, z_buf, part, out_a, in_a, out_c, in_c,
     eps_all, eps_rows, coef, out_h, in_h, field, first, second, third, result,
     load_sem, zs, zr, ys, yr, cs, cr, xas, xar, xcs, xcr, hs, hr, es, er, out_sem,
 ):
@@ -103,8 +103,8 @@
         jnp.where(same & (first_index < second_index), 1.0, 0.0), axis=0, keepdims=True
     )
     own = owners == brick.astype(F32)
-    slot_of = iota((BLOCK, 1), 0) & (MOST - 1)
-    slot_cell = jnp.zeros((BLOCK, 1), F32)
+    slot_of = iota((1, LANES), 1) & (MOST - 1)
+    slot_cell = jnp.zeros((1, LANES), F32)
     for j in range(MOST):
         cell = jnp.sum(
             jnp.where(own & (rank_across == j), cells, 0.0),
@@ -124,43 +124,33 @@
         group_down = group_down + jnp.where(position >= g * per, 1, 0)
     place = ((owner_down & 1) * groups + group_down) * CHIPS_Y + ((owner_down >> 1) & 3)
     place = (place * per + position - group_down * per) * BLOCK + rank_down.astype(jnp.int32)
-    pl.semaphore_wait(barrier, nz - 1 + 2 + 1 + 2 + 4)
-
-    for o in (-2, -1, 1, 2):
-        copy = pltpu.make_async_remote_copy(
-            src_ref=table_ref, dst_ref=eps_all.at[2 - o],
-            send_sem=es, recv_sem=er, **to({"brick": brick_off(o)})
-        )
-        copy.start()
-
-    fold[...] = jnp.where((iota((2 * nb, nb), 0) >> 1) == iota((2 * nb, nb), 1), 1.0, 0.0).astype(BF16)
+
+    fold[...] = jnp.where(iota((nb, 2 * nb), 0) == (iota((nb, 2 * nb), 1) >> 1), 1.0, 0.0).astype(
+        BF16
+    )
+    for s in range(2):
+        for n in range(parts):
+            hit = (iota((GROUP, LANES), 0) + n * GROUP == slot_column) & (
+                (iota((GROUP, LANES), 1) >> 3) == s
+            )
+            pick[s, n * GROUP : (n + 1) * GROUP, :] = jnp.where(hit, 1.0, 0.0).astype(BF16)
 
     half = nb // 2
-    row = iota((BLOCK, LANES), 0)
-    group_row = iota((BLOCK, GROUP), 0)
-
-    taken = jnp.zeros((BLOCK, 2 * nb), F32)
+    taken[...] = jnp.zeros_like(taken)
     for s in range(2):
         pltpu.make_async_copy(x_buf.at[s], x_buf.at[s], load_sem.at[s]).wait()
-
-        def take(n, taken):
-            start = pl.multiple_of(n * GROUP, GROUP)
-            pick = (iota((BLOCK, GROUP), 1) + start == slot_column) & (
-                (group_row >> 3) == s
-            )
-            return taken + lax.dot_general(
-                jnp.where(pick, 1.0, 0.0).astype(BF16),
-                x_buf[s, :, :, pl.ds(start, GROUP)].reshape(2 * nb, GROUP),
-                (((1,), (1,)), ((), ())), preferred_element_type=F32,
-            )
-
-        taken = lax.fori_loop(0, parts, take, taken)
-    keep = (iota((BLOCK, 2 * nb), 1) & 1) == slot_plane
-    taken = jnp.dot(
-        jnp.where(keep, taken, 0.0).astype(BF16), fold[...], preferred_element_type=F32
+        taken[...] += jnp.dot(
+            x_buf[s].reshape(2 * nb, plane), pick[s], preferred_element_type=F32
+        )
+    keep = (iota((2 * nb, LANES), 0) & 1) == slot_plane
+    folded = jnp.dot(
+        fold[...], jnp.where(keep, taken[...], 0.0).astype(BF16), preferred_element_type=F32
     )
-    mine = jnp.where(((row >> 2) & 1) == 0, taken[:, :half], taken[:, half:])
+    halves = [folded[half * i : half * (i + 1), :].T[:BLOCK, :] for i in range(2)]
+    mine = jnp.where(((iota((BLOCK, half), 0) >> 2) & 1) == 0, halves[0], halves[1])
     g_buf[core, y, 0] = mine.astype(BF16)
+
+    pl.semaphore_wait(barrier, nz - 1 + 2 + 1 + 2 + 4)
 
     def z_copy(i):
         away = (i + 1) // 2 if i % 2 else -(i // 2)
@@ -172,6 +162,13 @@
 
     for i in range(1, nz):
         z_copy(i).start()
+
+    for o in (-2, -1, 1, 2):
+        copy = pltpu.make_async_remote_copy(
+            src_ref=table_ref, dst_ref=eps_all.at[2 - o],
+            send_sem=es, recv_sem=er, **to({"brick": brick_off(o)})
+        )
+        copy.start()
 
     @pl.loop(0, sel.shape[1] // GROUP)
     def _(n):
@@ -575,7 +572,9 @@
             pltpu.VMEM((4 * npts, rows), BF16),
             pltpu.VMEM((4 * npts, LANES), F32),
             pltpu.VMEM((nb, 4 * nb), BF16),
-            pltpu.VMEM((2 * nb, nb), BF16),
+            pltpu.VMEM((nb, 2 * nb), BF16),
+            pltpu.VMEM((2, plane, LANES), BF16),
+            pltpu.VMEM((2 * nb, LANES), F32),
             pltpu.VMEM((2, 2 * npts, 2 * nb), BF16),
             pltpu.VMEM((2, 2, npts, plane), F32),
             pltpu.VMEM((2, chunks, 16, 2 * plane + LANES), jnp.int16),

time: 73.7 us -> 71.4 us (0.969)
  Pallas kernels: 69.9 us -> 67.6 us
    pallas_call x1, Pallas kernels: 69.9 us -> 67.6 us  [local(): pl.pallas_call(functools.partial(kernel, nz, nx), out_shape=[jax.ShapeDty...]
where the time goes in v6:
time: 71.4 us; the launch traced here: 71.2 us
  Pallas kernels  67.6 us (95%)
  local copies, waits for them, and re-layouts  1.59 us (2%)
  other arithmetic  1.43 us (2%)
    pallas_call x1, Pallas kernels, local(): pl.pallas_call(functools.partial(kernel, nz, nx), out_shape=[jax.ShapeDty...  67.6 us
    unnamed x2, local copies, waits for them, and re-layouts  1.59 us

profile of v6, /device:TPU:1, one launch (start us, length us, event | category | flops | bytes accessed | tf_op | source)
XLA Modules:
  0.0 71.2 jit_solution(1577429124791109926)
XLA Ops:
  0.6 0.7 pad_convert_fusion
  1.3 0.7 %pad_maximum_fusion.table_ref = f32[4,2048]{1,0:T(4,128)S(1)} fusion(f32[1,2048]{1,0:T(1,128)S(1)} %get-tuple-element.2, f32[1,2048]{1,0:T(1,128)S(1)} %get-tuple-element.3, f32[2,2048]{1,0:T(2,128)} %param.7), kind=kLoop, calls=%fused_computation | loop fusion | flops 16384 | bytes 65536 | tf_op jit(solution)/shard_map/concatenate | solution.py:558
  2.1 67.6 %shard_map.68 = (f32[32,2,2048]{2,1,0:T(2,128)S(1)}, f32[32,2,2048]{2,1,0:T(2,128)S(1)}) custom-call(f32[4,2048]{1,0:T(4,128)S(1)} %pad_maximum_fusion.table_ref, bf16[32,8,2,2048]{3,2,1,0:T(2,128)(2,1)} %bitcast.4, bf16[32,8,2,2048]{3,2,1,0:T(2,128)(2,1)} %bitcast.5), custom_call_target="tpu_custom_call" | custom-call | flops 1073741824 | bytes 5242880 | tf_op jit(solution)/shard_map/pallas_call | solution.py:562
  69.6 0.8 %copy.9 = f32[32,2,2048]{2,1,0:T(2,128)} copy(f32[32,2,2048]{2,1,0:T(2,128)S(1)} %get-tuple-element.6) | data formatting | bytes 1048576
  70.4 0.8 %copy.10 = f32[32,2,2048]{2,1,0:T(2,128)} copy(f32[32,2,2048]{2,1,0:T(2,128)S(1)} %get-tuple-element.7) | data formatting | bytes 1048576

commit v7 on v6

--- a/solution.py
+++ b/solution.py
@@ -38,7 +38,7 @@
     pair_ref, pot_ref,
     x_buf, g_buf, sel, found, spread, fold, pick, taken, z_buf, part, out_a, in_a, out_c, in_c,
     eps_all, eps_rows, coef, out_h, in_h, field, first, second, third, result,
-    load_sem, zs, zr, ys, yr, cs, cr, xas, xar, xcs, xcr, hs, hr, es, er, out_sem,
+    load_sem, zs, zr, ys, yr, cs, cr, fs, fr, xas, xar, xcs, xcr, hs, hr, es, er, out_sem,
 ):
     brick = lax.axis_index("brick")
     band = lax.axis_index("band")
@@ -72,11 +72,13 @@
     def _(dz):
         pl.semaphore_signal(barrier, 1, **to({"brick": brick_at(lax.rem(z + dz, nz), y, core)}))
 
-    for dy in (1, 3):
-        pl.semaphore_signal(
-            barrier, 1, **to({"brick": brick_at(z, lax.rem(y + dy, CHIPS_Y), core)})
-        )
-    pl.semaphore_signal(barrier, 1, **to({"brick": brick_at(z, y, 1 - core)}))
+    same_z = [(dy, dc) for dy in (2, 1, 3, 0) for dc in range(CORES) if (dy, dc) != (0, 0)]
+
+    def at_z(dy, dc):
+        return to({"brick": brick_at(z, lax.rem(y + dy, CHIPS_Y), 1 - core if dc else core)})
+
+    for dy, dc in same_z:
+        pl.semaphore_signal(barrier, 1, **at_z(dy, dc))
     for dx in (1, 3):
         pl.semaphore_signal(barrier, 1, **to({"band": band_off(dx)}))
     for o in (-2, -1, 1, 2):
@@ -150,7 +152,7 @@
     mine = jnp.where(((iota((BLOCK, half), 0) >> 2) & 1) == 0, halves[0], halves[1])
     g_buf[core, y, 0] = mine.astype(BF16)
 
-    pl.semaphore_wait(barrier, nz - 1 + 2 + 1 + 2 + 4)
+    pl.semaphore_wait(barrier, nz - 1 + len(same_z) + 2 + 4)
 
     def z_copy(i):
         away = (i + 1) // 2 if i % 2 else -(i // 2)
@@ -219,25 +221,37 @@
         return jnp.dot(sel[:, pl.ds(start, columns_of)], rows, preferred_element_type=F32)
 
     found[...] = jnp.zeros_like(found)
-    for step in range(groups + 3):
+    far = groups - 1
+
+    def far_copy(dy, dc):
+        block = g_buf.at[core, y, pl.ds(far * per, per)]
+        return pltpu.make_async_remote_copy(
+            src_ref=block, dst_ref=block, send_sem=fs.at[dc], recv_sem=fr.at[dc], **at_z(dy, dc)
+        )
+
+    for step in range(groups + 2):
         if step < groups:
             come = g_buf.at[core, y, pl.ds(max(1, step * per), per if step else per - 1)]
             pltpu.make_async_remote_copy(
                 src_ref=come, dst_ref=come, send_sem=zs, recv_sem=zr.at[step],
                 **to({"brick": brick_at(lax.rem(z + 1, nz), y, core)})
             ).wait_recv()
+        if step < far:
             y_copy(step, 0).start()
             y_copy(step, 1).start()
-        if 1 <= step <= groups:
+        if step == far:
+            for dy, dc in same_z:
+                far_copy(dy, dc).start()
+        if 1 <= step <= far:
             g = step - 1
             y_arrived(g, 0)
             y_copy(g, 2).start()
-        if 2 <= step <= groups + 1:
+        if 2 <= step <= far + 1:
             g = step - 2
             y_arrived(g, 1)
             core_copy(g).start()
             found[...] += find(core, g)
-        if step >= 3:
+        if 3 <= step <= far + 2:
             g = step - 3
             block = g_buf.at[1 - core, :, pl.ds(g * per, per)]
             pltpu.make_async_remote_copy(
@@ -245,6 +259,13 @@
                 **to({"brick": brick_at(z, y, 1 - core)})
             ).wait_recv()
             found[...] += find(1 - core, g)
+    for dc in range(CORES):
+        c = 1 - core if dc else core
+        block = g_buf.at[c, pl.ds(0, CHIPS_Y - 1 + dc), pl.ds(far * per, per)]
+        pltpu.make_async_remote_copy(
+            src_ref=block, dst_ref=block, send_sem=fs.at[dc], recv_sem=fr.at[dc], **at_z(1, 0)
+        ).wait_recv()
+        found[...] += find(c, far)
 
     for s in range(2):
         at_points = jnp.concatenate(
@@ -534,8 +555,11 @@
         ).wait_send()
 
     sent(g_buf.at[core, y, pl.ds(1, nz - 1)], zs, zr.at[0])
-    sent(g_buf.at[core, pl.ds(0, 3)], ys, yr.at[0, 0])
-    sent(g_buf.at[core], cs, cr.at[0])
+    near = pl.ds(0, far * per)
+    sent(g_buf.at[core, pl.ds(0, 3), near], ys, yr.at[0, 0])
+    sent(g_buf.at[core, :, near], cs, cr.at[0])
+    for dc in range(CORES):
+        sent(g_buf.at[core, pl.ds(0, 3 + dc), pl.ds(far * per, per)], fs.at[dc], fr.at[dc])
     sent(out_a, xas, xar.at[0, 0])
     sent(out_c, xcs, xcr.at[0])
     sent(in_h, hs, hr.at[0])
@@ -595,6 +619,7 @@
             dma, dma((groups,)),
             dma, dma((groups, 2)),
             dma, dma((groups,)),
+            dma((CORES,)), dma((CORES,)),
             dma, dma((2, chunks)),
             dma, dma((chunks,)),
             dma, dma((chunks,)),

time: 71.4 us -> 67 us (0.938)
  Pallas kernels: 67.6 us -> 63.2 us
    pallas_call x1, Pallas kernels: 67.6 us -> 63.2 us  [local(): pl.pallas_call(functools.partial(kernel, nz, nx), out_shape=[jax.ShapeDty...]
where the time goes in v7:
time: 67 us; the launch traced here: 66.8 us
  Pallas kernels  63.2 us (94%)
  local copies, waits for them, and re-layouts  1.59 us (2%)
  other arithmetic  1.43 us (2%)
    pallas_call x1, Pallas kernels, local(): pl.pallas_call(functools.partial(kernel, nz, nx), out_shape=[jax.ShapeDty...  63.2 us
    unnamed x2, local copies, waits for them, and re-layouts  1.59 us

profile of v7, /device:TPU:1, one launch (start us, length us, event | category | flops | bytes accessed | tf_op | source)
XLA Modules:
  0.0 66.8 jit_solution(5457233584200005028)
XLA Ops:
  0.6 0.7 %pad_convert_fusion = (f32[1,2048]{1,0:T(1,128)S(1)}, f32[1,2048]{1,0:T(1,128)S(1)}) fusion(s32[1,128]{1,0:T(1,128)} %bitcast.6, s32[1,128]{1,0:T(1,128)} %bitcast.7), kind=kLoop, calls=%fused_computation.1 | loop fusion | flops 4096 | bytes 17408 | tf_op jit(solution)/shard_map/convert_element_type | solution.py:580
  1.3 0.7 %pad_maximum_fusion.table_ref = f32[4,2048]{1,0:T(4,128)S(1)} fusion(f32[1,2048]{1,0:T(1,128)S(1)} %get-tuple-element.2, f32[1,2048]{1,0:T(1,128)S(1)} %get-tuple-element.3, f32[2,2048]{1,0:T(2,128)} %param.7), kind=kLoop, calls=%fused_computation | loop fusion | flops 16384 | bytes 65536 | tf_op jit(solution)/shard_map/concatenate | solution.py:582
  2.1 63.2 %shard_map.68 = (f32[32,2,2048]{2,1,0:T(2,128)S(1)}, f32[32,2,2048]{2,1,0:T(2,128)S(1)}) custom-call(f32[4,2048]{1,0:T(4,128)S(1)} %pad_maximum_fusion.table_ref, bf16[32,8,2,2048]{3,2,1,0:T(2,128)(2,1)} %bitcast.4, bf16[32,8,2,2048]{3,2,1,0:T(2,128)(2,1)} %bitcast.5), custom_call_target="tpu_custom_call" | custom-call | flops 1073741824 | bytes 5242880 | tf_op jit(solution)/shard_map/pallas_call | solution.py:586
  65.3 0.8 %copy.9 = f32[32,2,2048]{2,1,0:T(2,128)} copy(f32[32,2,2048]{2,1,0:T(2,128)S(1)} %get-tuple-element.6) | data formatting | bytes 1048576
  66.1 0.8 %copy.10 = f32[32,2,2048]{2,1,0:T(2,128)} copy(f32[32,2,2048]{2,1,0:T(2,128)S(1)} %get-tuple-element.7) | data formatting | bytes 1048576

commit v8 on v7

--- a/solution.py
+++ b/solution.py
@@ -189,18 +189,18 @@
     y_up, y_down = lax.rem(y + 1, CHIPS_Y), lax.rem(y + 3, CHIPS_Y)
 
     def y_copy(g, way):
-        odd = g % 2
-        source = y if way < 2 else (y_up if odd else y_down)
-        target = (y_up, y_down, y_down if odd else y_up)[way]
+        on = way == 2 and g == 0
+        source = y_down if on else y
+        target = (y_up, y_down, y_up if on else lax.rem(y + 2, CHIPS_Y))[way]
         part_of = g_buf.at[core, source, pl.ds(g * per, per)]
         return pltpu.make_async_remote_copy(
             src_ref=part_of, dst_ref=part_of, send_sem=ys,
-            recv_sem=yr.at[g, 0 if way == odd else 1],
+            recv_sem=yr.at[g, 0 if (g, way) == (0, 0) else 1],
             **to({"brick": brick_at(z, target, core)})
         )
 
     def y_arrived(g, n):
-        block = g_buf.at[core, pl.ds(0, n + 1), pl.ds(g * per, per)]
+        block = g_buf.at[core, pl.ds(0, 1 if n == 0 else 2 if g == 0 else 3), pl.ds(g * per, per)]
         pltpu.make_async_remote_copy(
             src_ref=block, dst_ref=block, send_sem=ys, recv_sem=yr.at[g, n],
             **to({"brick": brick_at(z, y_up, core)})
@@ -237,15 +237,14 @@
                 **to({"brick": brick_at(lax.rem(z + 1, nz), y, core)})
             ).wait_recv()
         if step < far:
-            y_copy(step, 0).start()
-            y_copy(step, 1).start()
+            for way in (0, 1) if step == 0 else (2, 0, 1):
+                y_copy(step, way).start()
         if step == far:
             for dy, dc in same_z:
                 far_copy(dy, dc).start()
-        if 1 <= step <= far:
-            g = step - 1
-            y_arrived(g, 0)
-            y_copy(g, 2).start()
+        if step == 1:
+            y_arrived(0, 0)
+            y_copy(0, 2).start()
         if 2 <= step <= far + 1:
             g = step - 2
             y_arrived(g, 1)

time: 67 us -> 67.1 us (level)
  no operation moved by 1% of the time
where the time goes in v8:
time: 67.1 us; the launch traced here: 66.9 us
  Pallas kernels  63.2 us (94%)
  local copies, waits for them, and re-layouts  1.59 us (2%)
  other arithmetic  1.43 us (2%)
    pallas_call x1, Pallas kernels, local(): pl.pallas_call(functools.partial(kernel, nz, nx), out_shape=[jax.ShapeDty...  63.2 us
    unnamed x2, local copies, waits for them, and re-layouts  1.59 us

profile of v8, /device:TPU:1, one launch (start us, length us, event | category | flops | bytes accessed | tf_op | source)
XLA Modules:
  0.0 66.9 jit_solution(5429265517195059340)
XLA Ops:
  0.6 0.7 %pad_convert_fusion = (f32[1,2048]{1,0:T(1,128)S(1)}, f32[1,2048]{1,0:T(1,128)S(1)}) fusion(s32[1,128]{1,0:T(1,128)} %bitcast.6, s32[1,128]{1,0:T(1,128)} %bitcast.7), kind=kLoop, calls=%fused_computation.1 | loop fusion | flops 4096 | bytes 17408 | tf_op jit(solution)/shard_map/convert_element_type | solution.py:579
  1.3 0.7 %pad_maximum_fusion.table_ref = f32[4,2048]{1,0:T(4,128)S(1)} fusion(f32[1,2048]{1,0:T(1,128)S(1)} %get-tuple-element.2, f32[1,2048]{1,0:T(1,128)S(1)} %get-tuple-element.3, f32[2,2048]{1,0:T(2,128)} %param.7), kind=kLoop, calls=%fused_computation | loop fusion | flops 16384 | bytes 65536 | tf_op jit(solution)/shard_map/concatenate | solution.py:581
  2.1 63.2 %shard_map.68 = (f32[32,2,2048]{2,1,0:T(2,128)S(1)}, f32[32,2,2048]{2,1,0:T(2,128)S(1)}) custom-call(f32[4,2048]{1,0:T(4,128)S(1)} %pad_maximum_fusion.table_ref, bf16[32,8,2,2048]{3,2,1,0:T(2,128)(2,1)} %bitcast.4, bf16[32,8,2,2048]{3,2,1,0:T(2,128)(2,1)} %bitcast.5), custom_call_target="tpu_custom_call" | custom-call | flops 1073741824 | bytes 5242880 | tf_op jit(solution)/shard_map/pallas_call | solution.py:585
  65.3 0.8 %copy.9 = f32[32,2,2048]{2,1,0:T(2,128)} copy(f32[32,2,2048]{2,1,0:T(2,128)S(1)} %get-tuple-element.6) | data formatting | bytes 1048576
  66.1 0.8 %copy.10 = f32[32,2,2048]{2,1,0:T(2,128)} copy(f32[32,2,2048]{2,1,0:T(2,128)S(1)} %get-tuple-element.7) | data formatting | bytes 1048576

commit v9 on v8

--- a/solution.py
+++ b/solution.py
@@ -249,15 +249,15 @@
             g = step - 2
             y_arrived(g, 1)
             core_copy(g).start()
-            found[...] += find(core, g)
-        if 3 <= step <= far + 2:
-            g = step - 3
-            block = g_buf.at[1 - core, :, pl.ds(g * per, per)]
-            pltpu.make_async_remote_copy(
-                src_ref=block, dst_ref=block, send_sem=cs, recv_sem=cr.at[g],
-                **to({"brick": brick_at(z, y, 1 - core)})
-            ).wait_recv()
-            found[...] += find(1 - core, g)
+    for g in range(far):
+        found[...] += find(core, g)
+    for g in range(far):
+        block = g_buf.at[1 - core, :, pl.ds(g * per, per)]
+        pltpu.make_async_remote_copy(
+            src_ref=block, dst_ref=block, send_sem=cs, recv_sem=cr.at[g],
+            **to({"brick": brick_at(z, y, 1 - core)})
+        ).wait_recv()
+        found[...] += find(1 - core, g)
     for dc in range(CORES):
         c = 1 - core if dc else core
         block = g_buf.at[c, pl.ds(0, CHIPS_Y - 1 + dc), pl.ds(far * per, per)]

time: 67.1 us -> 66.9 us (level)
  no operation moved by 1% of the time
where the time goes in v9:
time: 66.9 us; the launch traced here: 66.7 us
  Pallas kernels  63.1 us (94%)
  local copies, waits for them, and re-layouts  1.59 us (2%)
  other arithmetic  1.43 us (2%)
    pallas_call x1, Pallas kernels, local(): pl.pallas_call(functools.partial(kernel, nz, nx), out_shape=[jax.ShapeDty...  63.1 us
    unnamed x2, local copies, waits for them, and re-layouts  1.59 us

profile of v9, /device:TPU:1, one launch (start us, length us, event | category | flops | bytes accessed | tf_op | source)
XLA Modules:
  0.0 66.7 jit_solution(16321195992955112839)
XLA Ops:
  0.6 0.7 %pad_convert_fusion = (f32[1,2048]{1,0:T(1,128)S(1)}, f32[1,2048]{1,0:T(1,128)S(1)}) fusion(s32[1,128]{1,0:T(1,128)} %bitcast.6, s32[1,128]{1,0:T(1,128)} %bitcast.7), kind=kLoop, calls=%fused_computation.1 | loop fusion | flops 4096 | bytes 17408 | tf_op jit(solution)/shard_map/convert_element_type | solution.py:579
  1.3 0.7 %pad_maximum_fusion.table_ref = f32[4,2048]{1,0:T(4,128)S(1)} fusion(f32[1,2048]{1,0:T(1,128)S(1)} %get-tuple-element.2, f32[1,2048]{1,0:T(1,128)S(1)} %get-tuple-element.3, f32[2,2048]{1,0:T(2,128)} %param.7), kind=kLoop, calls=%fused_computation | loop fusion | flops 16384 | bytes 65536 | tf_op jit(solution)/shard_map/concatenate | solution.py:581
  2.1 63.1 %shard_map.68 = (f32[32,2,2048]{2,1,0:T(2,128)S(1)}, f32[32,2,2048]{2,1,0:T(2,128)S(1)}) custom-call(f32[4,2048]{1,0:T(4,128)S(1)} %pad_maximum_fusion.table_ref, bf16[32,8,2,2048]{3,2,1,0:T(2,128)(2,1)} %bitcast.4, bf16[32,8,2,2048]{3,2,1,0:T(2,128)(2,1)} %bitcast.5), custom_call_target="tpu_custom_call" | custom-call | flops 1073741824 | bytes 5242880 | tf_op jit(solution)/shard_map/pallas_call | solution.py:585
  65.1 0.8 %copy.9 = f32[32,2,2048]{2,1,0:T(2,128)} copy(f32[32,2,2048]{2,1,0:T(2,128)S(1)} %get-tuple-element.6) | data formatting | bytes 1048576
  65.9 0.8 %copy.10 = f32[32,2,2048]{2,1,0:T(2,128)} copy(f32[32,2,2048]{2,1,0:T(2,128)S(1)} %get-tuple-element.7) | data formatting | bytes 1048576
